TPU v7x, 256 devices: a whole 4x4x8 slice. The times are simulated.
256 devices in a mesh: dp: 2 (over x_hi), ctx: 32 (over z, x_lo, core), tensor: 4 (over y).
Axes of the slice: x: 4 (x_hi: 2, x_lo: 2; x = x_hi * 2 + x_lo), y: 4, z: 8, core: 2. Of those that a mesh axis runs over, the one named last changes fastest.
Arguments:
- queries: bfloat16 [4096, 2, 32, 128], P('ctx', 'dp', 'tensor'), may hold values from -200 to 200
- keys: bfloat16 [4096, 2, 4, 128], P('ctx', 'dp', 'tensor'), may hold values from -6 to 6
- values: bfloat16 [4096, 2, 4, 128], P('ctx', 'dp', 'tensor'), may hold values from -6 to 6
- segment_ids: int32 [64], P('ctx'), may hold values from 0 to 63, as said below
- feat_query: bfloat16 [32, 128, 64], P('tensor'), may hold values from -0.5 to 0.5
- feat_key: bfloat16 [32, 128, 64], P('tensor'), may hold values from -0.5 to 0.5
Outputs:
- student: bfloat16 [4096, 2, 32, 128], P('ctx', 'dp', 'tensor')
- grad_query: float32 [32, 128, 64], P('tensor')
- grad_key: float32 [32, 128, 64], P('tensor')
Inputs may be any that keep to these rules, and one draw needn't show every extreme that they name: `segment_ids`: entries 2 i and 2 i + 1 are the numbers i and 63 - i, in either order.
All inputs are finite; a program needn't handle non-finite values.
Results may differ from a plain program's by a relative error of at most 0.007.
Values may be sent and summed in bfloat16 or wider, within the bound.
No kernel may reach another device: no remote copies, remote signals or barrier semaphores. Data moves between devices by JAX's collectives and lax.ppermute only.
A program may use at most 128 MiB of HBM per device.

v0:
```python
import math

import jax
import jax.numpy as jnp
from jax import lax
from jax.sharding import PartitionSpec as P

NEGATIVE = -1e30
EXACT = lax.Precision.HIGHEST


def entering(shard, axis, combine, identity):
    length, index = (lax.axis_size(axis), lax.axis_index(axis))
    everything = jax.tree.map(lambda part: lax.all_gather(part, axis), shard)
    start = jax.tree.map(
        lambda part, zero: jnp.broadcast_to(jnp.asarray(zero, part.dtype), part.shape),
        shard,
        identity,
    )

    def entering_turn(k, before):
        reached = k < index
        new = combine(before, jax.tree.map(lambda part: part[k], everything))
        return jax.tree.map(lambda a, b: jnp.where(reached, a, b), new, before)

    return lax.fori_loop(0, length, entering_turn, start)


def carried_in(shard, axis, combine, identity):
    length, index = (lax.axis_size(axis), lax.axis_index(axis))
    everything = jax.tree.map(
        lambda part, kind: lax.all_gather(part.astype(kind), axis),
        shard,
        jax.tree.map(lambda a: jnp.bfloat16 if a.dtype == jnp.float32 else a.dtype, shard),
    )
    start = jax.tree.map(
        lambda part, zero: jnp.broadcast_to(jnp.asarray(zero, part.dtype), part.shape),
        shard,
        identity,
    )

    def carried_turn(k, before):
        at = length - 1 - k
        reached = at > index
        new = combine(
            before, jax.tree.map(lambda part, own: part[at].astype(own.dtype), everything, shard)
        )
        return jax.tree.map(lambda a, b: jnp.where(reached, a, b), new, before)

    return lax.fori_loop(0, length, carried_turn, start)


def feature_map(inputs, weight):
    projected = jnp.einsum("thd,hdf->thf", inputs, weight, precision=EXACT)
    return jnp.concatenate(
        [jax.nn.softmax(projected, axis=-1), jax.nn.softmax(-projected, axis=-1)], axis=-1
    )


def widen(inputs, head_count):
    return jnp.repeat(inputs, head_count // inputs.shape[1], axis=1)


def segment_states(phi_keys, value_rows):
    states = jnp.einsum("cthf,cthd->chfd", phi_keys, value_rows, precision=EXACT)
    return (states, jnp.sum(phi_keys, axis=1))


def segment_output(phi_queries, phi_keys, value_rows, prior_states, prior_sums):
    block_width = phi_queries.shape[1]
    causal = jnp.arange(block_width)[None, :] <= jnp.arange(block_width)[:, None]
    numerator = jnp.einsum("cthf,chfd->cthd", phi_queries, prior_states, precision=EXACT)
    denominator = jnp.einsum("cthf,chf->cth", phi_queries, prior_sums, precision=EXACT)
    weights = jnp.einsum("cthf,cshf->chts", phi_queries, phi_keys, precision=EXACT)
    weights = jnp.where(causal[None, None], weights, 0.0)
    numerator = numerator + jnp.einsum("chts,cshd->cthd", weights, value_rows, precision=EXACT)
    denominator = denominator + jnp.transpose(jnp.sum(weights, axis=3), (0, 2, 1))
    return numerator / denominator[..., None]


def add_all(earlier, later):
    return tuple((first_term + second_term for first_term, second_term in zip(earlier, later)))


def prefix_states(leading, trailing):
    zero_states = jnp.zeros_like(leading[0])
    zero_sums = jnp.zeros_like(leading[1])
    before_states, before_sums = entering(
        (leading[0], leading[1]), "ctx", add_all, (zero_states, zero_sums)
    )
    later_states, later_sums = carried_in(
        (trailing[0], trailing[1]), "ctx", add_all, (zero_states, zero_sums)
    )
    total_states, total_sums = (
        lax.psum(leading[0].astype(jnp.bfloat16), "ctx").astype(jnp.float32),
        lax.psum(leading[1].astype(jnp.bfloat16), "ctx").astype(jnp.float32),
    )
    after_states = total_states + later_states
    after_sums = total_sums + later_sums
    return ((before_states, before_sums), (after_states, after_sums))


def on_device(queries, keys, values, segment_ids, feat_query, feat_key):
    tokens_here = queries.shape[0]
    segment = tokens_here // 2
    head_count = queries.shape[2]
    head_dim = queries.shape[3]
    key_heads = keys.shape[2]
    group_size = head_count // key_heads
    feature_width = 2 * feat_query.shape[2]
    score_scale = head_dim ** (-0.5)
    offsets = jnp.arange(segment, dtype=jnp.int32)
    positions = (segment_ids[:, None] * segment + offsets[None, :]).reshape(-1)
    grouped = jnp.transpose(
        queries[:, 0].reshape(tokens_here, key_heads, group_size, head_dim), (1, 0, 2, 3)
    )
    grouped = grouped.reshape(key_heads, tokens_here * group_size, head_dim)
    query_positions = jnp.repeat(positions, group_size)
    weight_query = feat_query.astype(jnp.float32)
    weight_key = feat_key.astype(jnp.float32)
    start_state = (
        jnp.full((key_heads, tokens_here * group_size), NEGATIVE, jnp.float32),
        jnp.zeros((key_heads, tokens_here * group_size), jnp.float32),
        jnp.zeros((key_heads, tokens_here * group_size, head_dim), jnp.float32),
    )
    id_floats = segment_ids.astype(jnp.bfloat16)
    running = start_state
    key_portion = lax.all_gather(keys, "ctx", axis=0, tiled=True)
    value_portion = lax.all_gather(values, "ctx", axis=0, tiled=True)
    id_portion = lax.all_gather(id_floats, "ctx", axis=0, tiled=True)
    portion_rows = key_portion.shape[0]
    key_positions = (id_portion.astype(jnp.int32)[:, None] * segment + offsets[None, :]).reshape(-1)
    block_rows = math.gcd(portion_rows, 512)
    block_count = portion_rows // block_rows
    stacked = (
        key_portion[:, 0].reshape(block_count, block_rows, key_heads, head_dim),
        value_portion[:, 0].reshape(block_count, block_rows, key_heads, head_dim),
        key_positions.reshape(block_count, block_rows),
    )

    def one_block(running_state, blocked):
        key_block, value_block, position_block = blocked
        maxima, totals, accumulated = (running_state[0], running_state[1], running_state[2])
        new_maxima, new_totals, new_accumulated = ([], [], [])
        causal = position_block[None, :] <= query_positions[:, None]
        scores = (
            jnp.einsum("rd,kd->rk", grouped[0], key_block[:, 0], preferred_element_type=jnp.float32)
            * score_scale
        )
        block_top = jnp.max(jnp.where(causal, scores, NEGATIVE), axis=1)
        new_top = jnp.maximum(maxima[0], block_top)
        weights = jnp.where(causal, jnp.exp(scores - new_top[:, None]), 0.0)
        rescale = jnp.exp(maxima[0] - new_top)
        new_totals.append(totals[0] * rescale + jnp.sum(weights, axis=1))
        product = jnp.dot(
            weights.astype(jnp.bfloat16), value_block[:, 0], preferred_element_type=jnp.float32
        )
        new_accumulated.append(accumulated[0] * rescale[:, None] + product)
        new_maxima.append(new_top)
        result = (jnp.stack(new_maxima), jnp.stack(new_totals), jnp.stack(new_accumulated))
        return (result, None)

    running, unused = lax.scan(one_block, running, stacked)
    maxima, totals, accumulated = (running[0], running[1], running[2])
    teacher = (accumulated / totals[..., None]).reshape(
        key_heads, tokens_here, group_size, head_dim
    )
    teacher = jnp.transpose(teacher, (1, 0, 2, 3)).reshape(2, segment, head_count, head_dim)
    query_float = queries[:, 0].astype(jnp.float32)
    key_float = widen(keys[:, 0].astype(jnp.float32), head_count)
    value_float = widen(values[:, 0].astype(jnp.float32), head_count).reshape(
        2, segment, head_count, head_dim
    )
    swapped = segment_ids[0] > segment_ids[1]

    def key_features(weight_two):
        return feature_map(key_float, weight_two).reshape(2, segment, head_count, feature_width)

    def states_of(phi_keys):
        return segment_states(phi_keys, value_float)

    def output_of(weight_one, phi_keys, prior_states, prior_sums):
        phi_queries = feature_map(query_float, weight_one).reshape(
            2, segment, head_count, feature_width
        )
        return segment_output(phi_queries, phi_keys, value_float, prior_states, prior_sums)

    def split_pair(stacked_pair):
        return (
            jnp.where(swapped, stacked_pair[1], stacked_pair[0]),
            jnp.where(swapped, stacked_pair[0], stacked_pair[1]),
        )

    def arrange(leading_part, trailing_part):
        return jnp.stack(
            [
                jnp.where(swapped, trailing_part, leading_part),
                jnp.where(swapped, leading_part, trailing_part),
            ]
        )

    phi_keys, keys_back = jax.vjp(key_features, weight_key)
    (own_states, own_sums), states_back = jax.vjp(states_of, phi_keys)
    lead_states, trail_states = split_pair(own_states)
    lead_sums, trail_sums = split_pair(own_sums)
    prior_lead, prior_trail = prefix_states((lead_states, lead_sums), (trail_states, trail_sums))
    prior_states = arrange(prior_lead[0], prior_trail[0])
    prior_sums = arrange(prior_lead[1], prior_trail[1])
    student, output_back = jax.vjp(output_of, weight_query, phi_keys, prior_states, prior_sums)
    loss_scale = tokens_here * lax.axis_size("ctx") * lax.axis_size("dp")
    cotangent = (student - teacher) / loss_scale
    grad_query, grad_phi, grad_states, grad_sums = output_back(cotangent)
    grad_lead_states, grad_trail_states = split_pair(grad_states)
    grad_lead_sums, grad_trail_sums = split_pair(grad_sums)
    back_trail, back_lead = prefix_states(
        (grad_trail_states, grad_trail_sums), (grad_lead_states, grad_lead_sums)
    )
    (grad_phi_more,) = states_back(
        (arrange(back_lead[0], back_trail[0]), arrange(back_lead[1], back_trail[1]))
    )
    (grad_key,) = keys_back(grad_phi + grad_phi_more)
    grad_query, grad_key = lax.psum((grad_query, grad_key), ("dp", "ctx"))
    student_rows = student.reshape(tokens_here, 1, head_count, head_dim).astype(jnp.bfloat16)
    return (student_rows, grad_query, grad_key)


def solution(mesh):
    placed = (
        P("ctx", "dp", "tensor", None),
        P("ctx", "dp", "tensor", None),
        P("ctx", "dp", "tensor", None),
        P("ctx"),
        P("tensor", None, None),
        P("tensor", None, None),
    )
    return jax.shard_map(
        on_device,
        mesh=mesh,
        in_specs=placed,
        out_specs=(
            P("ctx", "dp", "tensor", None),
            P("tensor", None, None),
            P("tensor", None, None),
        ),
        check_vma=False,
    )
```

profile of v0, /device:TPU:16, one launch (start us, length us, event | category | flops | bytes accessed | tf_op | source)
XLA Modules:
  0.0 1147.7 jit_solution(15478779806954751656)
XLA Ops:
  20.0 40.1 %all_gather.44 = f32[32,8,128]{2,1,0:T(8,128)} all-gather(f32[1,8,128]{2,1,0:T(8,128)S(1)} %get-tuple-element.813), channel_id=1, replica_groups=mesh['dp'=2,'ctx'=32,'tensor'=4] {'ctx'}, dimensions={0}, use_global_device_ids=true | all-gather | bytes 135168 | tf_op jit(solution)/shard_map/all_gather | solution.py:14
  60.2 33.2 %all_gather.42 = bf16[32,8,128]{2,1,0:T(8,128)(2,1)} all-gather(bf16[1,8,128]{2,1,0:T(8,128)(2,1)S(1)} %select_convert_fusion.3), channel_id=1, replica_groups=mesh['dp'=2,'ctx'=32,'tensor'=4] {'ctx'}, dimensions={0}, use_global_device_ids=true | all-gather | bytes 67584 | tf_op jit(solution)/shard_map/all_gather | solution.py:32
  95.4 55.1 %all-reduce.2 = (bf16[8,128]{1,0:T(8,128)(2,1)}, bf16[64]{0:T(256)(128)(2,1)S(1)}) all-reduce(bf16[8,128]{1,0:T(8,128)(2,1)S(1)} %get-tuple-element.812, bf16[64]{0:T(256)(128)(2,1)S(1)} %dynamic-update-slice), channel_id=1, replica_groups=mesh['dp'=2,'ctx'=32,'tensor'=4] {'ctx'}, use_global_device_ids=true, to_apply=%region_14.15 | all-reduce | flops 1088 | bytes 4352 | tf_op jit(solution)/shard_map/psum | solution.py:96
  156.5 54.0 %while.85 = (s32[]{:T(128)}, f32[1,1024]{1,0:T(1,128)S(1)}, f32[1,1024]{1,0:T(1,128)S(1)}, f32[1,1024,128]{2,1,0:T(8,128)}, s32[8,512]{1,0:T(8,128)}, /*index=5*...) while((s32[]{:T(128)}, f32[1,1024]{1,0:T(1,128)S(1)}, ...), condition=%wide.region_19.20_spmd.clone, body=%wide.region_16.19_spmd.clone.sunk | while | flops 276044800 | bytes 12163780 | solution.py:163
  211.7 4.3 all-gather.7.cloned.1.call-done
  215.9 105.5 %while.83 = (s32[]{:T(128)}, f32[8,128,128]{2,1,0:T(8,128)}, f32[8,128]{1,0:T(8,128)}, s32[]{:T(128)}, bf16[32,8,128,128]{3,2,1,0:T(8,128)(2,1)}, /*index=5*/bf1...) while((s32[]{:T(128)}, f32[8,128,128]{2,1,0:T(8,128)}, ...), condition=%wide.region_7.8_spmd.clone, body=%wide.region_6.7_spmd.clone.sunk | while | flops 528392 | bytes 1321145 | solution.py:50
  219.1 2.0 add_select_fusion.16
  222.3 2.0 add_select_fusion.16
  225.6 2.0 add_select_fusion.16
  228.9 2.1 add_select_fusion.16
  232.3 2.0 add_select_fusion.16
  235.6 2.0 add_select_fusion.16
  238.9 2.1 add_select_fusion.16
  242.2 2.0 add_select_fusion.16
  245.5 2.0 add_select_fusion.16
  248.8 2.1 add_select_fusion.16
  252.1 2.0 add_select_fusion.16
  255.4 2.0 add_select_fusion.16
  258.7 2.0 add_select_fusion.16
  262.0 2.0 add_select_fusion.16
  265.3 2.0 add_select_fusion.16
  268.6 2.0 add_select_fusion.16
  271.9 2.0 add_select_fusion.16
  275.2 2.0 add_select_fusion.16
  278.5 2.0 add_select_fusion.16
  281.8 2.0 add_select_fusion.16
  285.1 2.1 add_select_fusion.16
  288.4 2.0 add_select_fusion.16
  291.8 2.0 add_select_fusion.16
  295.0 2.1 add_select_fusion.16
  298.4 2.0 add_select_fusion.16
  301.7 2.0 add_select_fusion.16
  305.0 2.1 add_select_fusion.16
  308.3 2.0 add_select_fusion.16
  311.6 2.0 add_select_fusion.16
  318.2 2.0 add_select_fusion.16
  321.5 61.3 %while.84 = (s32[]{:T(128)}, f32[8,128,128]{2,1,0:T(8,128)S(1)}, f32[8,128]{1,0:T(8,128)S(1)}, s32[]{:T(128)}, f32[32,8,128,128]{3,2,1,0:T(8,128)}, /*index=5*/f32[32,8,128]{2,1,0:T(8,128)}, s32[]{:T(128)}, s32[]{:T(128)}) while((s32[]{:T(128)}, f32[8,128,128]{2,1,0:T(8,128)S(1)}, f32[8,128]{1,0:T(8,128)S(1)}, s32[]{:T(128)}, ...), condition=%wide.region_9.10_spmd.clone, body=%wide.region_8.9_spmd.clone.sunk | while | flops 396292 | bytes 1585275 | solution.py:26
  383.8 159.0 %all-reduce.7.cloned.1.call-done = bf16[8,128,128]{2,1,0:T(8,128)(2,1)} async-done(((bf16[8,128,128]{2,1,0:T(8,128)(2,1)}), bf16[8,128,128]{2,1,0:T(8,128)(2,1)}) %all-reduce.7.cloned.1.call-update) | async-done | bytes 262160 | tf_op jit(solution)/shard_map/psum | solution.py:95
  552.2 3.3 fusion.29
  560.3 58.3 %psum.45 = bf16[8,128]{1,0:T(8,128)(2,1)S(1)} all-reduce(bf16[8,128]{1,0:T(8,128)(2,1)S(1)} %get-tuple-element.806), channel_id=1, replica_groups=mesh['dp'=2,'ctx'=32,'tensor'=4] {'ctx'}, use_global_device_ids=true, to_apply=%region_26.27 | all-reduce | flops 1024 | bytes 4096 | tf_op jit(solution)/shard_map/psum | solution.py:96
  618.6 32.9 %all_gather.51 = bf16[32,8,128]{2,1,0:T(8,128)(2,1)} all-gather(bf16[1,8,128]{2,1,0:T(8,128)(2,1)S(1)} %select_convert_fusion.2), channel_id=1, replica_groups=mesh['dp'=2,'ctx'=32,'tensor'=4] {'ctx'}, dimensions={0}, use_global_device_ids=true | all-gather | bytes 67584 | tf_op jit(solution)/shard_map/all_gather | solution.py:32
  651.5 36.7 %all_gather.49 = f32[32,8,128]{2,1,0:T(8,128)} all-gather(f32[1,8,128]{2,1,0:T(8,128)S(1)} %get-tuple-element.807), channel_id=1, replica_groups=mesh['dp'=2,'ctx'=32,'tensor'=4] {'ctx'}, dimensions={0}, use_global_device_ids=true | all-gather | bytes 135168 | tf_op jit(solution)/shard_map/all_gather | solution.py:14
  688.9 2.2 convolution_bitcast_fusion.4
  691.3 61.0 %while.87 = (s32[]{:T(128)}, f32[8,128,128]{2,1,0:T(8,128)S(1)}, f32[8,128]{1,0:T(8,128)S(1)}, s32[]{:T(128)}, bf16[32,8,128,128]{3,2,1,0:T(8,128)(2,1)}, /*inde...) while((s32[]{:T(128)}, f32[8,128,128]{2,1,0:T(8,128)S(1)}, ...), condition=%wide.region_28.29_spmd.clone, body=%wide.region_27.28_spmd.clone.sunk | while | flops 528392 | bytes 1321145 | solution.py:50
  752.2 61.3 %while.86 = (s32[]{:T(128)}, f32[8,128,128]{2,1,0:T(8,128)S(1)}, f32[8,128]{1,0:T(8,128)S(1)}, s32[]{:T(128)}, f32[32,8,128,128]{3,2,1,0:T(8,128)}, /*index=5*/f32[32,8,128]{2,1,0:T(8,128)}, s32[]{:T(128)}, s32[]{:T(128)}) while((s32[]{:T(128)}, f32[8,128,128]{2,1,0:T(8,128)S(1)}, f32[8,128]{1,0:T(8,128)S(1)}, s32[]{:T(128)}, ...), condition=%wide.region_25.26_spmd.clone, body=%wide.region_24.25_spmd.clone.sunk | while | flops 396292 | bytes 1585275 | solution.py:26
  813.5 136.1 %all-reduce.9.cloned.1.call-done = bf16[8,128,128]{2,1,0:T(8,128)(2,1)} async-done(((bf16[8,128,128]{2,1,0:T(8,128)(2,1)}), bf16[8,128,128]{2,1,0:T(8,128)(2,1)}) %all-reduce.9.cloned.1.call-update) | async-done | bytes 262160 | tf_op jit(solution)/shard_map/psum | solution.py:95
  950.7 2.1 fusion.30
  956.5 181.3 %all-reduce.11.cloned.1.call-done = (f32[8,128,64]{1,2,0:T(8,128)}, f32[8,128,64]{1,2,0:T(8,128)}) async-done(((f32[8,128,64]{1,2,0:T(8,128)}, f32[8,128,64]{1,2,0:T(8,128)}), (f32[8,128,64]{1,2,0:T(8,128)}, f32[8,128,64]{1,2,0:T(8,128)})) %all-reduce.11.cloned.1.call-update) | async-done | bytes 524304 | tf_op jit(solution)/shard_map/psum | solution.py:222
  (519 shorter events, 324.3 us)
Async XLA Ops:
  7.2 2.9 copy-start
  7.2 148.4 %all-gather.11.cloned.1.call-start = ((), (), s32[]{:S(2)}) async-start(), calls=%async_computation.3 | async-start | bytes 1081344 | tf_op jit(solution)/shard_map/all_gather | solution.py:128
  7.9 147.7 %all-gather.13.cloned.1.call-start = ((), (), s32[]{:S(2)}) async-start(), calls=%async_computation.4 | async-start | bytes 1081344 | tf_op jit(solution)/shard_map/all_gather | solution.py:129
  8.7 207.3 %all-gather.7.cloned.1.call-start = ((), (), s32[]{:S(2)}) async-start(), calls=%async_computation.1 | async-start | bytes 8650752 | tf_op jit(solution)/shard_map/all_gather | solution.py:32
  10.7 1.8 copy-start.24
  10.7 1.8 copy-start.37
  11.1 5.2 copy-start.27
  11.5 4.8 copy-start.29
  12.4 139.1 %copy-start.3 = (f32[128,8,128]{2,1,0:T(8,128)}, f32[128,8,128]{2,1,0:T(8,128)S(1)}, u32[]{:S(2)}) copy-start(f32[128,8,128]{2,1,0:T(8,128)S(1)} %copy.48) | copy-start | bytes 1572868
  16.3 2.6 copy-start.20
  16.3 2.6 copy-start.23
  17.1 304.4 %all-gather.9.cloned.1.call-start = ((), (), s32[]{:S(2)}) async-start(), calls=%async_computation.2 | async-start | bytes 17301504 | tf_op jit(solution)/shard_map/all_gather | solution.py:14
  18.1 524.8 %all-reduce.7.cloned.1.call-start = ((), (), s32[]{:S(2)}) async-start(), calls=%async_computation | async-start | bytes 524288 | tf_op jit(solution)/shard_map/psum | solution.py:95
  18.7 672.5 %all-gather.17.cloned.1.call-start = ((), (), s32[]{:S(2)}) async-start(), calls=%async_computation.6 | async-start | bytes 8650752 | tf_op jit(solution)/shard_map/all_gather | solution.py:32
  19.2 74.6 %copy-start.38 = (u32[256]{0:T(256)S(1)}, u32[256]{0:T(256)}, u32[]{:S(2)}) copy-start(u32[256]{0:T(256)} %constant.182) | copy-start | bytes 3076
  19.6 73.9 %copy-start.7 = (f32[128,8,64]{0,2,1:T(8,128)}, f32[128,8,64]{0,2,1:T(8,128)S(1)}, u32[]{:S(2)}) copy-start(f32[128,8,64]{0,2,1:T(8,128)S(1)} %get-tuple-element.844) | copy-start | bytes 786436
  19.6 131.0 %copy-start.31 = (f32[128,8]{0,1:T(8,128)}, f32[128,8]{0,1:T(8,128)S(1)}, u32[]{:S(2)}) copy-start(f32[128,8]{0,1:T(8,128)S(1)} %get-tuple-element.843) | copy-start | bytes 12292
  19.9 73.5 %copy-start.9 = (f32[128,8,64]{0,2,1:T(8,128)}, f32[128,8,64]{0,2,1:T(8,128)S(1)}, u32[]{:S(2)}) copy-start(f32[128,8,64]{0,2,1:T(8,128)S(1)} %get-tuple-element.846) | copy-start | bytes 786436
  19.9 130.6 %copy-start.33 = (f32[128,8]{0,1:T(8,128)}, f32[128,8]{0,1:T(8,128)S(1)}, u32[]{:S(2)}) copy-start(f32[128,8]{0,1:T(8,128)S(1)} %get-tuple-element.845) | copy-start | bytes 12292
  20.0 133.2 %copy-start.25 = (pred[64,64]{0,1:T(8,128)(4,1)}, pred[64,64]{0,1:T(8,128)(4,1)S(1)}, u32[]{:S(2)}) copy-start(pred[64,64]{0,1:T(8,128)(4,1)S(1)} %iota_compare_fusion) | copy-start | bytes 12292
  159.5 1.1 copy-start.13
  173.0 1.0 copy-start.13
  193.2 1.1 copy-start.13
  200.0 1.1 copy-start.13
  206.7 1.1 copy-start.13
  321.5 61.4 %copy-start.22 = (f32[8,128]{1,0:T(8,128)S(1)}, f32[8,128]{1,0:T(8,128)}, u32[]{:S(2)}) copy-start(f32[8,128]{1,0:T(8,128)} %get-tuple-element.583) | copy-start | bytes 12292
  321.5 61.4 %copy-start.36 = (bf16[8,128]{1,0:T(8,128)(2,1)S(1)}, bf16[8,128]{1,0:T(8,128)(2,1)}, u32[]{:S(2)}) copy-start(bf16[8,128]{1,0:T(8,128)(2,1)} %get-tuple-element.800) | copy-start | bytes 6148
  321.5 62.3 %copy-start.35 = (f32[2,8,64]{2,1,0:T(8,128)S(1)}, f32[2,8,64]{2,1,0:T(8,128)}, u32[]{:S(2)}) copy-start(f32[2,8,64]{2,1,0:T(8,128)} %get-tuple-element.847) | copy-start | bytes 12292
  321.5 221.4 %copy-start.2 = (f32[8,128,128]{2,1,0:T(8,128)S(1)}, f32[8,128,128]{2,1,0:T(8,128)}, u32[]{:S(2)}) copy-start(f32[8,128,128]{2,1,0:T(8,128)} %get-tuple-element.581) | copy-start | bytes 1572868
  382.8 161.1 %copy-start.17 = (f32[2,64,8,128]{3,1,2,0:T(8,128)S(1)}, f32[2,64,8,128]{3,1,2,0:T(8,128)}, u32[]{:S(2)}) copy-start(f32[2,64,8,128]{3,1,2,0:T(8,128)} %convolution_bitcast_fusion.2) | copy-start | bytes 1572868
  543.9 2.0 copy-start.11
  543.9 2.0 copy-start.12
  547.7 2.3 copy-start.34
  547.7 2.3 copy-start.32
  547.8 2.3 copy-start.30
  547.8 2.3 copy-start.28
  547.8 2.3 copy-start.26
  548.6 2.5 copy-start.4
  548.6 203.6 %all-gather.15.cloned.1.call-start = ((), (), s32[]{:S(2)}) async-start(), calls=%async_computation.5 | async-start | bytes 17301504 | tf_op jit(solution)/shard_map/all_gather | solution.py:14
  549.7 399.9 %all-reduce.9.cloned.1.call-start = ((), (), s32[]{:S(2)}) async-start(), calls=%async_computation.7 | async-start | bytes 524288 | tf_op jit(solution)/shard_map/psum | solution.py:95
  555.8 3.7 copy-start.10
  555.8 3.8 copy-start.8
  558.2 93.3 %copy-start.15 = (f32[128,8,64]{0,2,1:T(8,128)}, f32[128,8,64]{0,2,1:T(8,128)S(1)}, u32[]{:S(2)}) copy-start(f32[128,8,64]{0,2,1:T(8,128)S(1)} %copy.81) | copy-start | bytes 786436
  559.5 92.0 %copy-start.16 = (f32[128,8,64]{0,2,1:T(8,128)}, f32[128,8,64]{0,2,1:T(8,128)S(1)}, u32[]{:S(2)}) copy-start(f32[128,8,64]{0,2,1:T(8,128)S(1)} %copy.80) | copy-start | bytes 786436
  691.2 446.6 %all-reduce.11.cloned.1.call-start = ((), (), s32[]{:S(2)}) async-start(), calls=%async_computation.8 | async-start | bytes 1048576 | tf_op jit(solution)/shard_map/psum | solution.py:222
  953.2 1.1 copy-start.19
  953.6 2.0 copy-start.21
  954.2 186.9 %copy-start.1 = (bf16[8,128,64]{1,2,0:T(8,128)(2,1)S(1)}, bf16[8,128,64]{1,2,0:T(8,128)(2,1)}, u32[]{:S(2)}) copy-start(bf16[8,128,64]{1,2,0:T(8,128)(2,1)} %param.21) | copy-start | bytes 393220
  (14 other events, 12.1 us)
Sparse Core Ops, SparseCore 0:
  9.9 66.3 all-gather.10
  78.1 63.2 all-gather.12
  143.9 71.9 all-gather.6
  217.6 99.6 all-gather.8
  320.3 222.4 all-reduce.6
  548.7 73.1 all-gather.16
  623.9 100.6 all-gather.14
  727.4 222.1 all-reduce.8
  955.7 182.0 all-reduce.10
where the time goes:
time: 1160 us; the launch traced here: 1150 us
  waiting for transfers between devices  483 us (42%)
  other arithmetic  303 us (26%)
  blocking collectives  256 us (22%)
  matrix products  49.3 us (4%)
  local copies, waits for them, and re-layouts  37.5 us (3%)
  between operations  16.7 us (1%)
    psum x2, waiting for transfers between devices, prefix_states(): lax.psum(leading[0].astype(jnp.bfloat16), 'ctx').astype(jnp.float32)  295 us
    psum x1, waiting for transfers between devices, on_device(): grad_query, grad_key = lax.psum((grad_query, grad_key), ('dp', 'ctx'))  181 us
    select_n x128, other arithmetic, carried_turn(): return jax.tree.map(lambda a, b: jnp.where(reached, a, b), new, before)  166 us
    select_n x128, other arithmetic, entering_turn(): return jax.tree.map(lambda a, b: jnp.where(reached, a, b), new, before)  122 us
    psum x2, blocking collectives, prefix_states(): lax.psum(leading[1].astype(jnp.bfloat16), 'ctx').astype(jnp.float32)  113 us
    all_gather x2, blocking collectives, entering(): everything = jax.tree.map(lambda part: lax.all_gather(part, axis), shard)  76.9 us
    all_gather x2, blocking collectives, carried_in(): lax.all_gather(part.astype(kind), axis)  66.1 us
  transfers between devices with their start and end apart: 9, of which 4 were waited for; matrix products, arithmetic and copies ran while one was open for 32% of the time, Pallas kernels for 0%

commit v1 on v0

v1 whole, which is shorter than its diff:
```python
import math

import jax
import jax.numpy as jnp
from jax import lax
from jax.experimental import pallas as pl
from jax.experimental.pallas import tpu as pltpu
from jax.sharding import PartitionSpec as P

PLACES = 8
MEMBERS = 4
SEG = 64
HD = 128
FD = 64
PHI = 2 * FD
BLOCKS = 4
ROWS = 4 * SEG
HALF = 8 * SEG
AUG = HD + 16
LOSS = 1.0 / 8192.0
F32 = jnp.float32
BF16 = jnp.bfloat16
NN = (((1,), (0,)), ((), ()))
NT = (((1,), (1,)), ((), ()))


def dot(a, b, dims=NN):
    return lax.dot_general(a, b, dims, preferred_element_type=F32)


def split(array):
    high = array.astype(BF16)
    return high, (array - high.astype(F32)).astype(BF16)


def causal_mask(member, others, late):
    def turn(who):
        return 3 - who if late else who

    key = lax.broadcasted_iota(jnp.int32, (HALF, 1), 0)
    row = lax.broadcasted_iota(jnp.int32, (1, ROWS), 1)
    second = (key // SEG) % 2
    who = jnp.where(second == 0, member ^ others[0], member ^ others[1])
    key_at = (key // (2 * SEG)) * (4 * SEG) + turn(who) * SEG + key % SEG
    row_at = (row // SEG) * (4 * SEG) + turn(member) * SEG + row % SEG
    return key_at <= row_at


def features(projected):
    top = jnp.max(projected, axis=0, keepdims=True)
    bottom = jnp.min(projected, axis=0, keepdims=True)
    plus = jnp.exp(projected - top)
    minus = jnp.exp(bottom - projected)
    plus = plus * (1.0 / jnp.sum(plus, axis=0, keepdims=True))
    minus = minus * (1.0 / jnp.sum(minus, axis=0, keepdims=True))
    return jnp.concatenate([plus, minus], axis=0)


def features_back(phi, grad):
    term = phi * grad
    plus, minus = term[:FD], term[FD:]
    plus = plus - phi[:FD] * jnp.sum(plus, axis=0, keepdims=True)
    minus = minus - phi[FD:] * jnp.sum(minus, axis=0, keepdims=True)
    return plus - minus


def where_is(chunk):
    return (chunk, 0) if chunk < PLACES else (2 * PLACES - 1 - chunk, 1)


def block_rows(refs, block, columns):
    rows = []
    for chunk in range(4 * block, 4 * block + 4):
        place, late = where_is(chunk)
        rows += [ref[place, late, :, columns] for ref in refs]
    return jnp.concatenate(rows, axis=0)


KEY = slice(0, HD)
VALUE = slice(HD, 2 * HD)
QUERY = slice(2 * HD, 3 * HD)


def pack_kernel(ids_ref, q_ref, k_ref, v_ref, out_ref, wide):
    wide[...] = q_ref[...].astype(F32)
    swapped = ids_ref[0] > ids_ref[1]
    for late in range(2):
        start = jnp.where(swapped, SEG - SEG * late, SEG * late)
        rows = pl.ds(pl.multiple_of(start, SEG), SEG)
        pair = jnp.concatenate([k_ref[rows], v_ref[rows]], axis=1)
        for place in range(PLACES):
            out_ref[place, late, :, :2 * HD] = pair
            head = wide[pl.ds(start * PLACES + place, SEG, stride=PLACES)]
            out_ref[place, late, :, 2 * HD:] = head.astype(BF16)


def half_forward(refs, masks, queries, phi_q, wk, outs):
    top_ref, total_ref, acc_ref, num_ref, state_ref, phik_ref = outs
    scale = (HD ** -0.5) * math.log2(math.e)
    keys, values_t = [], []
    for block in range(BLOCKS):
        keys.append(block_rows(refs, block, KEY))
        value = block_rows(refs, block, VALUE).T
        values_t.append(jnp.concatenate([value, jnp.ones((AUG - HD, HALF), BF16)], axis=0))
    for block in range(BLOCKS):
        phi = features(dot(wk, keys[block], NT))
        phik_ref[block] = phi
        high, low = split(phi)
        state_ref[block] = dot(values_t[block], high, NT) + dot(values_t[block], low, NT)
        pair = dot(high.T, phi_q[block])
        high, low = split(jnp.where(masks[block // 2], pair, 0.0))
        num_ref[block] = dot(values_t[block], high) + dot(values_t[block], low)

        scores = [dot(keys[b], queries[block], NT) for b in range(block + 1)]
        scores[-1] = jnp.where(masks[block // 2], scores[-1], -1e30)
        top = jnp.max(scores[0], axis=0, keepdims=True)
        for s in scores[1:]:
            top = jnp.maximum(top, jnp.max(s, axis=0, keepdims=True))
        total, acc = 0.0, 0.0
        for b, s in enumerate(scores):
            weights = jnp.exp2(s * scale - top * scale)
            total = total + jnp.sum(weights, axis=0, keepdims=True)
            acc = acc + dot(values_t[b][:HD], weights.astype(BF16))
        top_ref[block] = top * scale
        total_ref[block] = total
        acc_ref[block] = acc


def first_kernel(at_ref, own_ref, core_ref, wq_ref, wk_ref, phiq_ref, *outs):
    place, member = at_ref[0], at_ref[1]
    masks = [causal_mask(member, (0, 1), late) for late in (False, True)]
    queries = [block_rows((own_ref,), b, QUERY) for b in range(BLOCKS)]
    phi_q = []
    for block in range(BLOCKS):
        phi = features(dot(wq_ref[place], queries[block], NT))
        phiq_ref[block] = phi
        phi_q.append(phi.astype(BF16))
    half_forward((own_ref, core_ref), masks, queries, phi_q, wk_ref[place], outs)


def second_kernel(
    at_ref, own_ref, x_ref, far_ref, wk_ref, phiq_ref,
    top_ref, total_ref, acc_ref, num_ref, state_ref,
    student_ref, phik_ref, prior_ref, dn_ref,
    top2_ref, total2_ref, acc2_ref, num2_ref, state2_ref,
):
    place, member = at_ref[0], at_ref[1]
    masks = [causal_mask(member, (2, 3), late) for late in (False, True)]
    queries = [block_rows((own_ref,), b, QUERY) for b in range(BLOCKS)]
    phi_q = [phiq_ref[block].astype(BF16) for block in range(BLOCKS)]
    outs = (top2_ref, total2_ref, acc2_ref, num2_ref, state2_ref, phik_ref)
    half_forward((x_ref, far_ref), masks, queries, phi_q, wk_ref[place], outs)
    prior = jnp.zeros((AUG, PHI), F32)
    for block in range(BLOCKS):
        top = jnp.maximum(top_ref[block], top2_ref[block])
        one = jnp.exp2(top_ref[block] - top)
        two = jnp.exp2(top2_ref[block] - top)
        total = total_ref[block] * one + total2_ref[block] * two
        teacher = (acc_ref[block] * one + acc2_ref[block] * two) * (1.0 / total)
        prior_ref[block] = prior
        numerator = num_ref[block] + num2_ref[block]
        if block > 0:
            high, low = split(prior)
            numerator = numerator + dot(
                jnp.concatenate([high, low], axis=1),
                jnp.concatenate([phi_q[block]] * 2, axis=0),
            )
        prior = prior + state_ref[block] + state2_ref[block]
        inverse = 1.0 / numerator[HD:HD + 1]
        y = numerator[:HD] * inverse
        d_num = (y - teacher) * (inverse * LOSS)
        d_den = -jnp.sum(d_num * y, axis=0, keepdims=True)
        high, low = split(d_num)
        den_high, den_low = split(d_den)
        index = lax.broadcasted_iota(jnp.int32, (AUG - HD, ROWS), 0)
        extra = jnp.where(
            index == 0, den_high.astype(F32), jnp.where(index == 1, den_low.astype(F32), 0.0)
        )
        dn_ref[block] = jnp.concatenate([high, low, extra.astype(BF16)], axis=0)
        rows = y.T.astype(BF16)
        for i in range(4):
            place, late = where_is(4 * block + i)
            student_ref[place, late] = rows[i * SEG:(i + 1) * SEG]


def backward_kernel(
    at_ref, own_ref, core_ref, x_ref, far_ref, phiq_ref, phik_ref, phik2_ref, prior_ref, dn_ref,
    grad_ref,
):
    member = at_ref[1]
    masks = [
        jnp.concatenate(
            [causal_mask(member, others, late) for others in ((0, 1), (2, 3))], axis=0
        )
        for late in (False, True)
    ]
    pieces = ((own_ref, core_ref), (x_ref, far_ref))

    def both(block, columns):
        return jnp.concatenate([block_rows(refs, block, columns) for refs in pieces], axis=0)

    grad_q = jnp.zeros((FD, HD), F32)
    grad_k = jnp.zeros((FD, HD), F32)
    later = jnp.zeros((PHI, HD), F32)
    later_den = jnp.zeros((PHI, 1), F32)
    for block in reversed(range(BLOCKS)):
        values = both(block, VALUE)
        keys = both(block, KEY)
        queries = block_rows((own_ref,), block, QUERY)
        phi_q = phiq_ref[block]
        phi_q16 = phi_q.astype(BF16)
        phi_k = jnp.concatenate([phik_ref[block], phik2_ref[block]], axis=1)
        grads = dn_ref[block]
        high = grads[:HD]
        d_den = (
            grads[2 * HD:2 * HD + 1].astype(F32) + grads[2 * HD + 1:2 * HD + 2].astype(F32)
        )
        pair = dot(values, high) + d_den
        pair = jnp.where(masks[block // 2], pair, 0.0).astype(BF16)
        phi_k_high, phi_k_low = split(phi_k)
        grad_phi = dot(phi_k_high, pair) + dot(phi_k_low, pair)
        if block > 0:
            prior = prior_ref[block].T
            top, low = split(prior[:, :HD])
            grad_phi = grad_phi + dot(
                jnp.concatenate([top, low], axis=1), jnp.concatenate([high, high], axis=0)
            )
            grad_phi = grad_phi + dot(top, grads[HD:2 * HD])
            grad_phi = grad_phi + prior[:, HD:HD + 1] * d_den
        projected = jnp.concatenate(split(features_back(phi_q, grad_phi)), axis=0)
        product = dot(projected, queries)
        grad_q = grad_q + product[:FD] + product[FD:]

        grad_phi = dot(phi_q16, pair, NT)
        if block < BLOCKS - 1:
            parts = jnp.concatenate(split(later), axis=1)
            doubled = jnp.concatenate([values, values], axis=1)
            grad_phi = grad_phi + dot(parts, doubled, NT) + later_den
        projected = jnp.concatenate(
            split(features_back(phi_k, grad_phi)), axis=0
        )
        product = dot(projected, keys)
        grad_k = grad_k + product[:FD] + product[FD:]
        if block > 0:
            terms = dot(phi_q16, grads, NT)
            later = later + terms[:, :HD] + terms[:, HD:2 * HD]
            later_den = later_den + terms[:, 2 * HD:2 * HD + 1] + terms[:, 2 * HD + 1:2 * HD + 2]
    grad_ref[0] = grad_q.astype(grad_ref.dtype)
    grad_ref[1] = grad_k.astype(grad_ref.dtype)


VMEM = pl.BlockSpec(memory_space=pltpu.VMEM)
SMEM = pl.BlockSpec(memory_space=pltpu.SMEM)
PARAMS = pltpu.CompilerParams(vmem_limit_bytes=40 * 1024 * 1024)
PARTIAL = [
    ((BLOCKS, 1, ROWS), F32),
    ((BLOCKS, 1, ROWS), F32),
    ((BLOCKS, HD, ROWS), F32),
    ((BLOCKS, AUG, ROWS), F32),
    ((BLOCKS, AUG, PHI), F32),
]
PHI_KEYS = ((BLOCKS, PHI, HALF), F32)


def call(kernel, name, outs, args, scratch=(), flops=0):
    return pl.pallas_call(
        kernel,
        out_shape=[jax.ShapeDtypeStruct(*out) for out in outs],
        in_specs=[SMEM] + [VMEM] * (len(args) - 1),
        out_specs=[VMEM] * len(outs),
        scratch_shapes=[pltpu.VMEM(*s) for s in scratch],
        compiler_params=PARAMS,
        cost_estimate=pl.CostEstimate(flops=flops, bytes_accessed=0, transcendentals=0),
        name=name,
    )(*args)


def on_device(queries, keys, values, segment_ids, feat_query, feat_key):
    spot = lax.axis_index("ctx")
    place, member = spot // MEMBERS, spot % MEMBERS
    z_groups = [[j + MEMBERS * k for k in range(PLACES)] for j in range(MEMBERS)]

    def swap(array, relative):
        return lax.ppermute(array, "ctx", [(i, i ^ relative) for i in range(32)])

    def along_z(array):
        return lax.all_to_all(array, "ctx", 0, 0, axis_index_groups=z_groups)

    swapped = segment_ids[0] > segment_ids[1]
    at = jnp.stack([place, member]).astype(jnp.int32)

    (sent,) = call(
        pack_kernel, "pack",
        [((PLACES, 2, SEG, 3 * HD), BF16)],
        (
            segment_ids,
            queries.reshape(2 * SEG * PLACES, HD),
            keys.reshape(2 * SEG, HD),
            values.reshape(2 * SEG, HD),
        ),
        [((2 * SEG * PLACES, HD), F32)],
    )
    own = along_z(sent)
    mine = own[..., :2 * HD]
    beside = swap(mine, 2)
    core = swap(mine, 1)
    far = swap(beside, 1)

    wq = jnp.transpose(feat_query, (0, 2, 1))
    wk = jnp.transpose(feat_key, (0, 2, 1))

    phi_q, *first = call(
        first_kernel, "first_half",
        [((BLOCKS, PHI, ROWS), F32)] + PARTIAL + [PHI_KEYS],
        (at, own, core, wq, wk),
        flops=5 * 10 ** 9,
    )
    student, phi_k2, prior, grads = call(
        second_kernel, "second_half",
        [
            ((PLACES, 2, SEG, HD), BF16),
            PHI_KEYS,
            ((BLOCKS, AUG, PHI), F32),
            ((BLOCKS, 2 * HD + 16, ROWS), BF16),
        ],
        (at, own, beside, far, wk, phi_q, *first[:5]),
        PARTIAL,
        flops=5 * 10 ** 9,
    )
    (grad,) = call(
        backward_kernel, "backward",
        [((2, FD, HD), BF16)],
        (at, own, core, beside, far, phi_q, first[5], phi_k2, prior, grads),
        flops=5 * 10 ** 9,
    )

    sum_groups = [
        [32 * d + MEMBERS * k + j for d in range(2) for j in range(MEMBERS)]
        for k in range(PLACES)
    ]
    shares = lax.all_to_all(
        jnp.broadcast_to(grad, (8,) + grad.shape), ("dp", "ctx"), 0, 0,
        axis_index_groups=sum_groups,
    )
    share = jnp.sum(shares.astype(F32), axis=0).astype(BF16)
    share = jnp.broadcast_to(share, (PLACES,) + share.shape)
    whole = along_z(jnp.concatenate([student, share], axis=-1))
    student = whole[..., :HD]
    student = jnp.where(swapped, student[:, ::-1], student)
    student = jnp.transpose(student, (1, 2, 0, 3)).reshape(2 * SEG, 1, PLACES, HD)
    grads = jnp.transpose(whole[..., HD:], (1, 0, 3, 2)).astype(F32)
    return student, grads[0], grads[1]


def solution(mesh):
    placed = (
        P("ctx", "dp", "tensor", None),
        P("ctx", "dp", "tensor", None),
        P("ctx", "dp", "tensor", None),
        P("ctx"),
        P("tensor", None, None),
        P("tensor", None, None),
    )
    return jax.shard_map(
        on_device,
        mesh=mesh,
        in_specs=placed,
        out_specs=(
            P("ctx", "dp", "tensor", None),
            P("tensor", None, None),
            P("tensor", None, None),
        ),
        check_vma=False,
    )
```

time: 1160 us -> 102 us (0.09)
  waiting for transfers between devices: 483 us -> 25.8 us
  other arithmetic: 303 us -> 1.14 us
  blocking collectives: 256 us -> 43.1 us
  matrix products: 49.3 us -> 0 us
  local copies, waits for them, and re-layouts: 37.5 us -> 5.54 us
  Pallas kernels: 0 us -> 17.3 us
  between operations: 16.7 us -> 2.03 us
    psum x3 -> x0, waiting for transfers between devices: 476 us -> none  [the longest x2 295 us: prefix_states(): lax.psum(leading[0].astype(jnp.bfloat16), 'ctx').astype(jnp.float32)]
    select_n x256 -> x1, other arithmetic: 289 us -> 0.06 us  [on_device(): student = jnp.where(swapped, student[:, ::-1], student)]
    all_gather x4 -> x0, blocking collectives: 143 us -> none  [the longest x2 76.9 us: entering(): everything = jax.tree.map(lambda part: lax.all_gather(part, axis), shard)]
    psum x2 -> x0, blocking collectives: 113 us -> none  [prefix_states(): lax.psum(leading[1].astype(jnp.bfloat16), 'ctx').astype(jnp.float32)]
    dot_general x32 -> x0, matrix products: 49.3 us -> none  [the longest x8 14.3 us: one_block(): jnp.dot(weights.astype(jnp.bfloat16), value_block[:, 0], preferred_elemen...]
    all_to_all x0 -> x2, blocking collectives: none -> 43.1 us  [the longest x1 31.4 us: along_z(): return lax.all_to_all(array, 'ctx', 0, 0, axis_index_groups=z_groups)]
    pallas_call x0 -> x4, Pallas kernels: none -> 17.3 us  [call(): pl.pallas_call(kernel, out_shape=[jax.ShapeDtypeStruct(*out) for out in o...]
    all_to_all x0 -> x1, waiting for transfers between devices: none -> 15.4 us  [along_z(): return lax.all_to_all(array, 'ctx', 0, 0, axis_index_groups=z_groups)]
  transfers between devices with their start and end apart: 9 -> 4, of which waited for: 4 -> 2; matrix products, arithmetic and copies ran while one was open for 32% -> 1% of each run, Pallas kernels for 0% -> 5%
where the time goes in v1:
time: 102 us; the launch traced here: 100 us
  blocking collectives  43.1 us (42%)
  waiting for transfers between devices  25.8 us (25%)
  Pallas kernels  17.3 us (17%)
  local copies, waits for them, and re-layouts  5.54 us (5%)
  starting transfers between devices  5.07 us (5%)
  between operations  2.03 us (2%)
  other arithmetic  1.14 us (1%)
    all_to_all x1, blocking collectives, along_z(): return lax.all_to_all(array, 'ctx', 0, 0, axis_index_groups=z_groups)  31.4 us
    pallas_call x4, Pallas kernels, call(): pl.pallas_call(kernel, out_shape=[jax.ShapeDtypeStruct(*out) for out in o...  17.3 us
    all_to_all x1, waiting for transfers between devices, along_z(): return lax.all_to_all(array, 'ctx', 0, 0, axis_index_groups=z_groups)  15.4 us
    all_to_all x1, blocking collectives, on_device(): lax.all_to_all(jnp.broadcast_to(grad, (8,) + grad.shape), ('dp', 'ctx'),...  11.7 us
    ppermute x3, waiting for transfers between devices, swap(): return lax.ppermute(array, 'ctx', [(i, i ^ relative) for i in range(32)])  10.4 us
    unnamed x13, local copies, waits for them, and re-layouts  4 us
    all_to_all x1, starting transfers between devices, along_z(): return lax.all_to_all(array, 'ctx', 0, 0, axis_index_groups=z_groups)  3.49 us
  transfers between devices with their start and end apart: 4, of which 2 were waited for; matrix products, arithmetic and copies ran while one was open for 1% of the time, Pallas kernels for 5%

profile of v1, /device:TPU:16, one launch (start us, length us, event | category | flops | bytes accessed | tf_op | source)
XLA Modules:
  0.0 100.1 jit_solution(8531319698390350294)
XLA Ops:
  0.6 0.0 copy-start.3
  0.6 0.6 copy-done.3
  1.3 0.0 copy-start
  1.3 0.9 copy-done
  2.2 0.0 copy-start.1
  2.2 0.8 copy-done.1
  3.0 0.0 copy-start.2
  3.0 0.8 copy-done.2
  3.8 0.7 pack.1
  4.5 31.4 %all_to_all.15.own_ref = bf16[8,2,64,384]{3,2,1,0:T(8,128)(2,1)S(1)} all-to-all(bf16[8,2,64,384]{3,2,1,0:T(8,128)(2,1)S(1)} %pack.1), channel_id=1, replica_groups={{0,16,32,48,64,80,96,112},{4,20,36,52,68,84,100,116},{8,24,40,56,72,88,..., dimensions={0} | all-to-all | bytes 1572864 | tf_op jit(solution)/shard_map/all_to_all | solution.py:287
  35.8 0.0 copy-start.4
  35.8 0.0 copy-start.5
  35.9 1.6 %collective-permute-start = (bf16[8,2,64,256]{3,2,1,0:T(8,128)(2,1)S(1)}, bf16[8,2,64,256]{3,2,1,0:T(8,128)(2,1)S(1)}, u32[]{:S(2)}, u32[]{:S(2)}) collective-permute-start(bf16[8,2,64,256]{3,2,1,0:T(8,128)(2,1)S(1)} %slice.28), channel_id=1, source_target_pairs={{0,8},{4,12},{8,0},{12,4},{16,24},{20,28},{24,16},{28,20},{32,40},... | collective-permute-start | bytes 1572872 | tf_op jit(solution)/shard_map/ppermute | solution.py:284
  37.5 0.0 collective-permute-start.2
  37.5 10.4 %collective-permute-done.x_ref = bf16[8,2,64,256]{3,2,1,0:T(8,128)(2,1)S(1)} collective-permute-done((bf16[8,2,64,256]{3,2,1,0:T(8,128)(2,1)S(1)}, bf16[8,2,64,256]{3,2,1,0:T(8,128)(2,1)S(1)}, u32[]{:S(2)}, u32[]{:S(2)}) %collective-permute-start) | collective-permute-done | bytes 524320 | tf_op jit(solution)/shard_map/ppermute | solution.py:284
  47.9 0.0 collective-permute-start.1
  47.9 0.1 pad_add_fusion.at_ref
  47.9 0.0 collective-permute-done.2.core_ref
  47.9 0.0 copy-done.4
  47.9 0.0 copy-done.5
  47.9 5.4 %first_half.1 = (f32[4,128,256]{2,1,0:T(8,128)S(1)}, f32[4,1,256]{2,1,0:T(1,128)S(1)}, f32[4,1,256]{2,1,0:T(1,128)S(1)}, f32[4,128,256]{2,1,0:T(8,128)S(1)}, f32...) custom-call(s32[2]{0:T(128)S(1)} %pad_add_fusion.at_ref, ...), custom_call_target="tpu_custom_call" | custom-call | flops 5000000000 | tf_op jit(solution)/shard_map/first_half/pallas_call | solution.py:266
  53.3 0.0 collective-permute-done.1.far_ref
  53.3 5.6 %second_half.1 = (bf16[8,2,64,128]{3,2,1,0:T(8,128)(2,1)S(1)}, f32[4,128,512]{2,1,0:T(8,128)S(1)}, f32[4,144,128]{2,1,0:T(8,128)S(1)}, bf16[4,272,256]{2,1,0:T(8,128)(2,1)S(1)}) custom-call(s32[2]{0:T(128)S(1)} %pad_add_fusion.at_ref, bf16[8,2,64,384]{3,2,1,0:T(8,128)(2,1)S(1)} %all_to_all.15.own_ref, ...), custom_call_target="tpu_custom_call" | custom-call | flops 5000000000 | tf_op jit(solution)/shard_map/second_half/pallas_call | solution.py:266
  58.9 5.7 %backward.1 = bf16[2,64,128]{2,1,0:T(8,128)(2,1)S(1)} custom-call(s32[2]{0:T(128)S(1)} %pad_add_fusion.at_ref, bf16[8,2,64,384]{3,2,1,0:T(8,128)(2,1)S(1)} %all_to_all.15.own_ref, bf16[8,2,64,256]{3,2,1,0:T(8,128)(2,1)S(1)} %collective-permute-done.2.core_ref, bf16[8,2,64,256]{3,2,1,0:T(8,128)(2,1)S(1)} %collective-permute-done.x_ref, ...), custom_call_target="tpu_custom_call" | custom-call | flops 5000000000 | tf_op jit(solution)/shard_map/backward/pallas_call | solution.py:266
  64.6 0.1 broadcast_in_dim.6
  64.7 11.7 %all_to_all.16 = bf16[8,2,64,128]{3,2,1,0:T(8,128)(2,1)S(1)} all-to-all(bf16[8,2,64,128]{3,2,1,0:T(8,128)(2,1)S(1)} %broadcast_in_dim.6), channel_id=1, replica_groups={{0,4,8,12,128,132,136,140},{16,20,24,28,144,148,152,156},{32,36,40,44,1..., dimensions={0} | all-to-all | bytes 524288 | tf_op jit(solution)/shard_map/all_to_all | solution.py:341
  76.5 0.9 pad_maximum_fusion
  77.4 3.5 %all-to-all-start.2 = ((bf16[8,2,64,256]{3,2,1,0:T(8,128)(2,1)}), bf16[8,2,64,256]{3,2,1,0:T(8,128)(2,1)S(1)}, u32[]{:S(2)}, u32[]{:S(2)}) async-start(bf16[8,2,64,256]{3,2,1,0:T(8,128)(2,1)} %pad_maximum_fusion), calls=%async_computation.2 | async-start | bytes 1048576 | tf_op jit(solution)/shard_map/all_to_all | solution.py:287
  80.9 0.6 fusion
  82.8 15.4 %all-to-all-done.2 = bf16[8,2,64,256]{3,2,1,0:T(8,128)(2,1)S(1)} async-done(((bf16[8,2,64,256]{3,2,1,0:T(8,128)(2,1)}), bf16[8,2,64,256]{3,2,1,0:T(8,128)(2,1)S(1)}, u32[]{:S(2)}, u32[]{:S(2)}) %all-to-all-start.2) | async-done | bytes 524320 | tf_op jit(solution)/shard_map/all_to_all | solution.py:287
  98.2 0.1 convert_bitcast_fusion
  98.3 0.1 reverse_select_fusion
  98.4 0.9 copy.10
  99.2 0.8 slice_bitcast_fusion
  (3 shorter events, 0.1 us)
Async XLA Ops:
  0.6 0.7 copy-start.3
  1.3 0.9 copy-start
  2.2 0.8 copy-start.1
  3.0 0.8 copy-start.2
  35.8 12.1 %copy-start.4 = (bf16[8,128,64]{1,2,0:T(8,128)(2,1)S(1)}, bf16[8,128,64]{1,2,0:T(8,128)(2,1)}, u32[]{:S(2)}) copy-start(bf16[8,128,64]{1,2,0:T(8,128)(2,1)} %param.10) | copy-start | bytes 393220
  35.8 12.1 %copy-start.5 = (bf16[8,128,64]{1,2,0:T(8,128)(2,1)S(1)}, bf16[8,128,64]{1,2,0:T(8,128)(2,1)}, u32[]{:S(2)}) copy-start(bf16[8,128,64]{1,2,0:T(8,128)(2,1)} %param.11) | copy-start | bytes 393220
  35.9 12.0 %collective-permute-start = (bf16[8,2,64,256]{3,2,1,0:T(8,128)(2,1)S(1)}, bf16[8,2,64,256]{3,2,1,0:T(8,128)(2,1)S(1)}, u32[]{:S(2)}, u32[]{:S(2)}) collective-permute-start(bf16[8,2,64,256]{3,2,1,0:T(8,128)(2,1)S(1)} %slice.28), channel_id=1, source_target_pairs={{0,8},{4,12},{8,0},{12,4},{16,24},{20,28},{24,16},{28,20},{32,40},... | collective-permute-start | bytes 1572872 | tf_op jit(solution)/shard_map/ppermute | solution.py:284
  37.5 10.5 %collective-permute-start.2 = (bf16[8,2,64,256]{3,2,1,0:T(8,128)(2,1)S(1)}, bf16[8,2,64,256]{3,2,1,0:T(8,128)(2,1)S(1)}, u32[]{:S(2)}, u32[]{:S(2)}) collective-permute-start(bf16[8,2,64,256]{3,2,1,0:T(8,128)(2,1)S(1)} %slice.28), channel_id=1, source_target_pairs={{0,4},{4,0},{8,12},{12,8},{16,20},{20,16},{24,28},{28,24},{32,36},... | collective-permute-start | bytes 1572872 | tf_op jit(solution)/shard_map/ppermute | solution.py:284
  47.9 5.5 %collective-permute-start.1 = (bf16[8,2,64,256]{3,2,1,0:T(8,128)(2,1)S(1)}, bf16[8,2,64,256]{3,2,1,0:T(8,128)(2,1)S(1)}, u32[]{:S(2)}, u32[]{:S(2)}) collective-permute-start(bf16[8,2,64,256]{3,2,1,0:T(8,128)(2,1)S(1)} %collective-permute-done.x_ref), channel_id=1, source_target_pairs={{0,4},{4,0},{8,12},{12,8},{16,20},{20,16},{24,28},{28,24},{32,36},... | collective-permute-start | bytes 1572872 | tf_op jit(solution)/shard_map/ppermute | solution.py:284
  77.4 20.8 %all-to-all-start.2 = ((bf16[8,2,64,256]{3,2,1,0:T(8,128)(2,1)}), bf16[8,2,64,256]{3,2,1,0:T(8,128)(2,1)S(1)}, u32[]{:S(2)}, u32[]{:S(2)}) async-start(bf16[8,2,64,256]{3,2,1,0:T(8,128)(2,1)} %pad_maximum_fusion), calls=%async_computation.2 | async-start | bytes 1048576 | tf_op jit(solution)/shard_map/all_to_all | solution.py:287

commit v2 on v1

v2 whole, which is shorter than its diff:
```python
import math

import jax
import jax.numpy as jnp
from jax import lax
from jax.experimental import pallas as pl
from jax.experimental.pallas import tpu as pltpu
from jax.sharding import PartitionSpec as P

PLACES = 8
MEMBERS = 4
SEG = 64
HD = 128
FD = 64
PHI = 2 * FD
BLOCKS = 4
ROWS = 4 * SEG
HALF = 8 * SEG
AUG = HD + 16
LOSS = 1.0 / 8192.0
F32 = jnp.float32
BF16 = jnp.bfloat16
NN = (((1,), (0,)), ((), ()))
NT = (((1,), (1,)), ((), ()))


def dot(a, b, dims=NN):
    return lax.dot_general(a, b, dims, preferred_element_type=F32)


def split(array):
    high = array.astype(BF16)
    return high, (array - high.astype(F32)).astype(BF16)


def causal_mask(member, others, late):
    def turn(who):
        return 3 - who if late else who

    key = lax.broadcasted_iota(jnp.int32, (HALF, 1), 0)
    row = lax.broadcasted_iota(jnp.int32, (1, ROWS), 1)
    second = (key // SEG) % 2
    who = jnp.where(second == 0, member ^ others[0], member ^ others[1])
    key_at = (key // (2 * SEG)) * (4 * SEG) + turn(who) * SEG + key % SEG
    row_at = (row // SEG) * (4 * SEG) + turn(member) * SEG + row % SEG
    return key_at <= row_at


def features(projected):
    top = jnp.max(projected, axis=0, keepdims=True)
    bottom = jnp.min(projected, axis=0, keepdims=True)
    plus = jnp.exp(projected - top)
    minus = jnp.exp(bottom - projected)
    plus = plus * (1.0 / jnp.sum(plus, axis=0, keepdims=True))
    minus = minus * (1.0 / jnp.sum(minus, axis=0, keepdims=True))
    return jnp.concatenate([plus, minus], axis=0)


def features_back(phi, grad):
    term = phi * grad
    plus, minus = term[:FD], term[FD:]
    plus = plus - phi[:FD] * jnp.sum(plus, axis=0, keepdims=True)
    minus = minus - phi[FD:] * jnp.sum(minus, axis=0, keepdims=True)
    return plus - minus


def where_is(chunk):
    return (chunk, 0) if chunk < PLACES else (2 * PLACES - 1 - chunk, 1)


def block_rows(refs, block, columns):
    rows = []
    for chunk in range(4 * block, 4 * block + 4):
        place, late = where_is(chunk)
        rows += [ref[place, late, :, columns] for ref in refs]
    return jnp.concatenate(rows, axis=0)


KEY = slice(0, HD)
VALUE = slice(HD, 2 * HD)
QUERY = slice(0, HD)


def pack_kernel(ids_ref, q_ref, k_ref, v_ref, out_ref, outq_ref, flag_ref, ids, q16, wide, k16, v16, sems):
    copies = [
        pltpu.make_async_copy(source, target, sems.at[i])
        for i, (source, target) in enumerate(
            ((ids_ref, ids), (k_ref, k16), (v_ref, v16), (q_ref, q16))
        )
    ]
    for copy in copies:
        copy.start()
    for copy in copies[:3]:
        copy.wait()
    swapped = ids[0] > ids[1]
    flag_ref[0] = jnp.where(swapped, 1, 0)

    def half_rows(late):
        start = jnp.where(swapped, SEG - SEG * late, SEG * late)
        return pl.multiple_of(start, SEG)

    for late in range(2):
        rows = pl.ds(half_rows(late), SEG)
        pair = jnp.concatenate([k16[rows], v16[rows]], axis=1)
        for place in range(PLACES):
            out_ref[place, late] = pair
    copies[3].wait()
    wide[...] = q16[...].astype(F32)
    for late in range(2):
        for place in range(PLACES):
            rows = pl.ds(half_rows(late) * PLACES + place, SEG, stride=PLACES)
            outq_ref[place, late] = wide[rows].astype(BF16)


def tie_kernel(value_ref, token_ref, out_ref):
    pass


def pair_kernel(one_ref, two_ref, out_ref):
    out_ref[...] = (one_ref[...] + two_ref[...]).astype(BF16)


def share_kernel(a_ref, b_ref, c_ref, d_ref, student_ref, out_ref):
    one = a_ref[...].astype(F32) + b_ref[...].astype(F32)
    two = c_ref[...].astype(F32) + d_ref[...].astype(F32)
    total = (one + two).astype(BF16)
    for place in range(PLACES):
        out_ref[place, :, :, :HD] = student_ref[place]
        out_ref[place, :, :, HD:] = total


def finish_kernel(flag_ref, whole_ref, student_ref, gq_ref, gk_ref, wide):
    for place in range(PLACES):
        gq_ref[place] = whole_ref[place, 0, :, HD:].astype(F32)
        gk_ref[place] = whole_ref[place, 1, :, HD:].astype(F32)
    swapped = flag_ref[0] == 1
    for late in range(2):
        start = pl.multiple_of(jnp.where(swapped, SEG - SEG * late, SEG * late), SEG)
        for place in range(PLACES):
            rows = pl.ds(start * PLACES + place, SEG, stride=PLACES)
            wide[rows] = whole_ref[place, late, :, :HD].astype(F32)
    student_ref[...] = wide[...].astype(BF16)


def half_forward(refs, masks, queries, phi_q, wk, outs):
    top_ref, total_ref, acc_ref, num_ref, state_ref, phik_ref = outs
    scale = (HD ** -0.5) * math.log2(math.e)
    keys, values_t = [], []
    for block in range(BLOCKS):
        keys.append(block_rows(refs, block, KEY))
        value = block_rows(refs, block, VALUE).T
        values_t.append(jnp.concatenate([value, jnp.ones((AUG - HD, HALF), BF16)], axis=0))
    for block in range(BLOCKS):
        phi = features(dot(wk, keys[block], NT))
        phik_ref[block] = phi
        phi16 = phi.astype(BF16)
        state_ref[block] = dot(values_t[block], phi16, NT)
        pair = dot(phi16.T, phi_q[block])
        pair = jnp.where(masks[block // 2], pair, 0.0)
        if block == 0:
            high, low = split(pair)
            num_ref[block] = dot(values_t[block], high) + dot(values_t[block], low)
        else:
            num_ref[block] = dot(values_t[block], pair.astype(BF16))

        scores = [dot(keys[b], queries[block], NT) for b in range(block + 1)]
        scores[-1] = jnp.where(masks[block // 2], scores[-1], -1e30)
        top = jnp.max(scores[0], axis=0, keepdims=True)
        for s in scores[1:]:
            top = jnp.maximum(top, jnp.max(s, axis=0, keepdims=True))
        total, acc = 0.0, 0.0
        for b, s in enumerate(scores):
            weights = jnp.exp2(s * scale - top * scale)
            total = total + jnp.sum(weights, axis=0, keepdims=True)
            acc = acc + dot(values_t[b][:HD], weights.astype(BF16))
        top_ref[block] = top * scale
        total_ref[block] = total
        acc_ref[block] = acc


def first_kernel(at_ref, rows_ref, own_ref, core_ref, wq_ref, wk_ref, phiq_ref, *outs):
    place, member = at_ref[0], at_ref[1]
    masks = [causal_mask(member, (0, 1), late) for late in (False, True)]
    queries = [block_rows((rows_ref,), b, QUERY) for b in range(BLOCKS)]
    phi_q = []
    for block in range(BLOCKS):
        phi = features(dot(wq_ref[place], queries[block], NT))
        phiq_ref[block] = phi
        phi_q.append(phi.astype(BF16))
    half_forward((own_ref, core_ref), masks, queries, phi_q, wk_ref[place], outs)


def second_kernel(
    at_ref, rows_ref, x_ref, far_ref, wk_ref, phiq_ref,
    top_ref, total_ref, acc_ref, num_ref, state_ref,
    student_ref, phik_ref, prior_ref, dn_ref,
    top2_ref, total2_ref, acc2_ref, num2_ref, state2_ref,
):
    place, member = at_ref[0], at_ref[1]
    masks = [causal_mask(member, (2, 3), late) for late in (False, True)]
    queries = [block_rows((rows_ref,), b, QUERY) for b in range(BLOCKS)]
    phi_q = [phiq_ref[block].astype(BF16) for block in range(BLOCKS)]
    outs = (top2_ref, total2_ref, acc2_ref, num2_ref, state2_ref, phik_ref)
    half_forward((x_ref, far_ref), masks, queries, phi_q, wk_ref[place], outs)
    prior = jnp.zeros((AUG, PHI), F32)
    for block in range(BLOCKS):
        top = jnp.maximum(top_ref[block], top2_ref[block])
        one = jnp.exp2(top_ref[block] - top)
        two = jnp.exp2(top2_ref[block] - top)
        total = total_ref[block] * one + total2_ref[block] * two
        teacher = (acc_ref[block] * one + acc2_ref[block] * two) * (1.0 / total)
        prior_ref[block] = prior
        numerator = num_ref[block] + num2_ref[block]
        if block > 0:
            numerator = numerator + dot(prior.astype(BF16), phi_q[block])
        prior = prior + state_ref[block] + state2_ref[block]
        inverse = 1.0 / numerator[HD:HD + 1]
        y = numerator[:HD] * inverse
        d_num = (y - teacher) * (inverse * LOSS)
        d_den = -jnp.sum(d_num * y, axis=0, keepdims=True)
        den_high, den_low = split(d_den)
        index = lax.broadcasted_iota(jnp.int32, (AUG - HD, ROWS), 0)
        extra = jnp.where(
            index == 0, den_high.astype(F32), jnp.where(index == 1, den_low.astype(F32), 0.0)
        )
        dn_ref[block] = jnp.concatenate([d_num.astype(BF16), extra.astype(BF16)], axis=0)
        rows = y.T.astype(BF16)
        for i in range(4):
            place, late = where_is(4 * block + i)
            student_ref[place, late] = rows[i * SEG:(i + 1) * SEG]


def backward_kernel(
    at_ref, rows_ref, own_ref, core_ref, x_ref, far_ref, phiq_ref, phik_ref, phik2_ref, prior_ref, dn_ref,
    grad_ref,
):
    member = at_ref[1]
    masks = [
        jnp.concatenate(
            [causal_mask(member, others, late) for others in ((0, 1), (2, 3))], axis=0
        )
        for late in (False, True)
    ]
    pieces = ((own_ref, core_ref), (x_ref, far_ref))

    def both(block, columns):
        return jnp.concatenate([block_rows(refs, block, columns) for refs in pieces], axis=0)

    def project(phi, grad, rows, exact):
        back = features_back(phi, grad)
        if not exact:
            return dot(back.astype(BF16), rows)
        product = dot(jnp.concatenate(split(back), axis=0), rows)
        return product[:FD] + product[FD:]

    grad_q = jnp.zeros((FD, HD), F32)
    grad_k = jnp.zeros((FD, HD), F32)
    later = jnp.zeros((PHI, AUG), F32)
    for block in reversed(range(BLOCKS)):
        first = block == 0
        values = both(block, VALUE)
        keys = both(block, KEY)
        queries = block_rows((rows_ref,), block, QUERY)
        phi_q = phiq_ref[block]
        phi_q16 = phi_q.astype(BF16)
        phi_k = jnp.concatenate([phik_ref[block], phik2_ref[block]], axis=1)
        grads = dn_ref[block]
        d_den = grads[HD:HD + 1].astype(F32) + grads[HD + 1:HD + 2].astype(F32)
        pair = dot(values, grads[:HD]) + d_den
        pair = jnp.where(masks[block // 2], pair, 0.0).astype(BF16)
        if first:
            grad_phi = dot(jnp.concatenate(split(phi_k), axis=0), pair)
            grad_phi = grad_phi[:PHI] + grad_phi[PHI:]
        else:
            prior = prior_ref[block].T
            grad_phi = dot(phi_k.astype(BF16), pair) + dot(prior.astype(BF16), grads)
        grad_q = grad_q + project(phi_q, grad_phi, queries, first)

        if block == BLOCKS - 1:
            grad_phi = dot(phi_q16, pair, NT)
        else:
            grad_phi = dot(
                jnp.concatenate([phi_q16, later[:, :HD].astype(BF16)], axis=1),
                jnp.concatenate([pair, values], axis=1),
                NT,
            )
            grad_phi = grad_phi + (later[:, HD:HD + 1] + later[:, HD + 1:HD + 2])
        grad_k = grad_k + project(phi_k, grad_phi, keys, first)
        if not first:
            later = later + dot(phi_q16, grads, NT)
    grad_ref[0] = grad_q.astype(grad_ref.dtype)
    grad_ref[1] = grad_k.astype(grad_ref.dtype)


VMEM = pl.BlockSpec(memory_space=pltpu.VMEM)
SMEM = pl.BlockSpec(memory_space=pltpu.SMEM)
ANY = pl.BlockSpec(memory_space=pl.ANY)
PARAMS = pltpu.CompilerParams(vmem_limit_bytes=8 * 1024 * 1024)
PARTIAL = [
    ((BLOCKS, 1, ROWS), F32),
    ((BLOCKS, 1, ROWS), F32),
    ((BLOCKS, HD, ROWS), F32),
    ((BLOCKS, AUG, ROWS), F32),
    ((BLOCKS, AUG, PHI), F32),
]
PHI_KEYS = ((BLOCKS, PHI, HALF), F32)


def call(kernel, name, outs, args, scratch=(), flops=0, smem=True):
    return pl.pallas_call(
        kernel,
        out_shape=[jax.ShapeDtypeStruct(*out) for out in outs],
        in_specs=[SMEM if smem else VMEM] + [VMEM] * (len(args) - 1),
        out_specs=[VMEM] * len(outs),
        scratch_shapes=[pltpu.VMEM(*s) for s in scratch],
        compiler_params=PARAMS,
        cost_estimate=pl.CostEstimate(flops=flops, bytes_accessed=0, transcendentals=0),
        name=name,
    )(*args)


def tied(array, token):
    return pl.pallas_call(
        tie_kernel,
        out_shape=jax.ShapeDtypeStruct(array.shape, array.dtype),
        in_specs=[ANY, ANY],
        out_specs=ANY,
        input_output_aliases={0: 0},
        compiler_params=pltpu.CompilerParams(vmem_limit_bytes=1024 * 1024),
        name="tie",
    )(array, token)


def on_device(queries, keys, values, segment_ids, feat_query, feat_key):
    spot = lax.axis_index("ctx")
    place, member = spot // MEMBERS, spot % MEMBERS
    z_groups = [[j + MEMBERS * k for k in range(PLACES)] for j in range(MEMBERS)]

    def swap(array, relative):
        return lax.ppermute(array, "ctx", [(i, i ^ relative) for i in range(32)])

    def along_z(array):
        return lax.all_to_all(array, "ctx", 0, 0, axis_index_groups=z_groups)

    at = jnp.stack([place, member]).astype(jnp.int32)

    sent, sent_q, flag = pl.pallas_call(
        pack_kernel,
        out_shape=[
            jax.ShapeDtypeStruct((PLACES, 2, SEG, 2 * HD), BF16),
            jax.ShapeDtypeStruct((PLACES, 2, SEG, HD), BF16),
            jax.ShapeDtypeStruct((1,), jnp.int32),
        ],
        in_specs=[ANY] * 4,
        out_specs=[VMEM, VMEM, SMEM],
        scratch_shapes=[
            pltpu.SMEM((2,), jnp.int32),
            pltpu.VMEM((2 * SEG * PLACES, HD), BF16),
            pltpu.VMEM((2 * SEG * PLACES, HD), F32),
            pltpu.VMEM((2 * SEG, HD), BF16),
            pltpu.VMEM((2 * SEG, HD), BF16),
            pltpu.SemaphoreType.DMA((4,)),
        ],
        compiler_params=pltpu.CompilerParams(vmem_limit_bytes=62 * 1024 * 1024),
        name="pack",
    )(
        segment_ids,
        queries.reshape(2 * SEG * PLACES, HD),
        keys.reshape(2 * SEG, HD),
        values.reshape(2 * SEG, HD),
    )
    own = along_z(sent)
    beside = swap(own, 2)
    core = swap(own, 1)
    rows = along_z(tied(sent_q, own))

    wq = jnp.transpose(feat_query, (0, 2, 1))
    wk = jnp.transpose(feat_key, (0, 2, 1))

    phi_q, *first = call(
        first_kernel, "first_half",
        [((BLOCKS, PHI, ROWS), F32)] + PARTIAL + [PHI_KEYS],
        (at, rows, own, core, wq, wk),
        flops=5 * 10 ** 9,
    )
    beside = tied(beside, rows)
    far = swap(beside, 1)
    student, phi_k2, prior, grads = call(
        second_kernel, "second_half",
        [
            ((PLACES, 2, SEG, HD), BF16),
            PHI_KEYS,
            ((BLOCKS, AUG, PHI), F32),
            ((BLOCKS, AUG, ROWS), BF16),
        ],
        (at, rows, beside, far, wk, phi_q, *first[:5]),
        PARTIAL,
        flops=5 * 10 ** 9,
    )
    (grad,) = call(
        backward_kernel, "backward",
        [((2, FD, HD), F32)],
        (at, rows, own, core, beside, far, phi_q, first[5], phi_k2, prior, grads),
        flops=5 * 10 ** 9,
    )

    def swap_wide(array, relative):
        pairs = [(i, i ^ relative) for i in range(64)]
        return lax.ppermute(array, ("dp", "ctx"), pairs)

    (pair,) = call(
        pair_kernel, "pair", [((2, FD, HD), BF16)], (grad, swap(grad, 1)), smem=False
    )
    (share,) = call(
        share_kernel, "share", [((PLACES, 2, SEG, 2 * HD), BF16)],
        (pair, swap_wide(pair, 2), swap_wide(pair, 32), swap_wide(pair, 34), student),
        smem=False,
    )
    whole = along_z(share)
    student, grad_query, grad_key = pl.pallas_call(
        finish_kernel,
        out_shape=[
            jax.ShapeDtypeStruct((2 * SEG * PLACES, HD), BF16),
            jax.ShapeDtypeStruct((PLACES, FD, HD), F32),
            jax.ShapeDtypeStruct((PLACES, FD, HD), F32),
        ],
        in_specs=[SMEM, VMEM],
        out_specs=[VMEM] * 3,
        scratch_shapes=[pltpu.VMEM((2 * SEG * PLACES, HD), F32)],
        compiler_params=PARAMS,
        name="finish",
    )(flag, whole)
    student = student.reshape(2 * SEG, 1, PLACES, HD)
    return student, jnp.transpose(grad_query, (0, 2, 1)), jnp.transpose(grad_key, (0, 2, 1))


def solution(mesh):
    placed = (
        P("ctx", "dp", "tensor", None),
        P("ctx", "dp", "tensor", None),
        P("ctx", "dp", "tensor", None),
        P("ctx"),
        P("tensor", None, None),
        P("tensor", None, None),
    )
    return jax.shard_map(
        on_device,
        mesh=mesh,
        in_specs=placed,
        out_specs=(
            P("ctx", "dp", "tensor", None),
            P("tensor", None, None),
            P("tensor", None, None),
        ),
        check_vma=False,
    )
```

time: 102 us -> 88.4 us (0.87); the launches traced: 100 us -> 88.1 us
  waiting for transfers between devices: 25.8 us -> 14.9 us
  local copies, waits for them, and re-layouts: 5.54 us -> 0.01 us
  starting transfers between devices: 5.07 us -> 9.78 us
  blocking collectives: 43.1 us -> 44.9 us
  between operations: 2.03 us -> 0.74 us
  other arithmetic: 1.14 us -> 0.07 us
    all_to_all x1 -> x2, blocking collectives: 31.4 us -> 44.9 us  [along_z(): return lax.all_to_all(array, 'ctx', 0, 0, axis_index_groups=z_groups)]
    all_to_all x1 -> x0, blocking collectives: 11.7 us -> none  [on_device(): lax.all_to_all(jnp.broadcast_to(grad, (8,) + grad.shape), ('dp', 'ctx'),...]
    ppermute x3 -> x4, waiting for transfers between devices: 10.4 us -> 0.91 us  [swap(): return lax.ppermute(array, 'ctx', [(i, i ^ relative) for i in range(32)])]
    all_to_all x1, waiting for transfers between devices: 15.4 us -> 10.3 us  [along_z(): return lax.all_to_all(array, 'ctx', 0, 0, axis_index_groups=z_groups)]
    ppermute x0 -> x3, starting transfers between devices: none -> 4.18 us  [swap_wide(): return lax.ppermute(array, ('dp', 'ctx'), pairs)]
    unnamed x13 -> x4, local copies, waits for them, and re-layouts: 4 us -> 0.01 us
    ppermute x0 -> x3, waiting for transfers between devices: none -> 3.74 us  [swap_wide(): return lax.ppermute(array, ('dp', 'ctx'), pairs)]
    pallas_call x0 -> x4, Pallas kernels: none -> 3.35 us  [the longest x1 1.91 us: on_device(): pl.pallas_call(pack_kernel, out_shape=[jax.ShapeDtypeStruct((PLACES, 2, S...]
  transfers between devices with their start and end apart: 4 -> 8, of which waited for: 2 -> 4; matrix products, arithmetic and copies ran while one was open for 1% -> 0% of each run, Pallas kernels for 5% -> 5%
where the time goes in v2:
time: 88.4 us; the launch traced here: 88.1 us
  blocking collectives  44.9 us (51%)
  Pallas kernels  17.6 us (20%)
  waiting for transfers between devices  14.9 us (17%)
  starting transfers between devices  9.78 us (11%)
    all_to_all x2, blocking collectives, along_z(): return lax.all_to_all(array, 'ctx', 0, 0, axis_index_groups=z_groups)  44.9 us
    pallas_call x5, Pallas kernels, call(): pl.pallas_call(kernel, out_shape=[jax.ShapeDtypeStruct(*out) for out in o...  14.3 us
    all_to_all x1, waiting for transfers between devices, along_z(): return lax.all_to_all(array, 'ctx', 0, 0, axis_index_groups=z_groups)  10.3 us
    ppermute x3, starting transfers between devices, swap_wide(): return lax.ppermute(array, ('dp', 'ctx'), pairs)  4.18 us
    ppermute x3, waiting for transfers between devices, swap_wide(): return lax.ppermute(array, ('dp', 'ctx'), pairs)  3.74 us
    all_to_all x1, starting transfers between devices, along_z(): return lax.all_to_all(array, 'ctx', 0, 0, axis_index_groups=z_groups)  3.41 us
    ppermute x4, starting transfers between devices, swap(): return lax.ppermute(array, 'ctx', [(i, i ^ relative) for i in range(32)])  2.18 us
    pallas_call x1, Pallas kernels, on_device(): pl.pallas_call(pack_kernel, out_shape=[jax.ShapeDtypeStruct((PLACES, 2, S...  1.91 us
  transfers between devices with their start and end apart: 8, of which 4 were waited for; matrix products, arithmetic and copies ran while one was open for 0% of the time, Pallas kernels for 5%

profile of v2, /device:TPU:16, one launch (start us, length us, event | category | flops | bytes accessed | tf_op | source)
XLA Modules:
  0.0 88.1 jit_solution(2078267312142999572)
XLA Ops:
  0.6 1.9 %pack.1 = (bf16[8,2,64,256]{3,2,1,0:T(8,128)(2,1)}, bf16[8,2,64,128]{3,2,1,0:T(8,128)(2,1)}, s32[1]{0:T(128)}) custom-call(s32[2]{0:T(128)} %ids_ref.1, bf16[1024,128]{1,0:T(8,128)(2,1)} %bitcast.15, bf16[128,128]{1,0:T(8,128)(2,1)} %bitcast.16, bf16[128,128]{1,0:T(8,128)(2,1)} %bitcast.17), custom_call_target="tpu_custom_call" | custom-call | tf_op jit(solution)/shard_map/pack/pallas_call | solution.py:347
  2.5 26.0 %all_to_all.15.token_ref.own_ref = bf16[8,2,64,256]{3,2,1,0:T(8,128)(2,1)S(1)} all-to-all(bf16[8,2,64,256]{3,2,1,0:T(8,128)(2,1)} %get-tuple-element.22), channel_id=1, replica_groups={{0,16,32,48,64,80,96,112},{4,20,36,52,68,84,100,116},{8,24,40,56,72,88,..., dimensions={0} | all-to-all | bytes 1048576 | tf_op jit(solution)/shard_map/all_to_all | solution.py:343
  28.5 1.5 %collective-permute-start.1 = (bf16[8,2,64,256]{3,2,1,0:T(8,128)(2,1)S(1)}, bf16[8,2,64,256]{3,2,1,0:T(8,128)(2,1)S(1)}, u32[]{:S(2)}, u32[]{:S(2)}) collective-permute-start(bf16[8,2,64,256]{3,2,1,0:T(8,128)(2,1)S(1)} %all_to_all.15.token_ref.own_ref), channel_id=1, source_target_pairs={{0,8},{4,12},{8,0},{12,4},{16,24},{20,28},{24,16},{28,20},{32,40},... | collective-permute-start | bytes 1572872 | tf_op jit(solution)/shard_map/ppermute | solution.py:340
  30.0 3.4 %all-to-all-start.1 = ((bf16[8,2,64,128]{3,2,1,0:T(8,128)(2,1)}), bf16[8,2,64,128]{3,2,1,0:T(8,128)(2,1)S(1)}, u32[]{:S(2)}, u32[]{:S(2)}) async-start(bf16[8,2,64,128]{3,2,1,0:T(8,128)(2,1)} %tie.2), calls=%async_computation.1 | async-start | bytes 524288 | tf_op jit(solution)/shard_map/all_to_all | solution.py:343
  33.4 0.1 collective-permute-start
  33.6 0.0 copy-start
  33.6 0.0 copy-start.1
  33.6 10.3 %all-to-all-done.1.token_ref.rows_ref = bf16[8,2,64,128]{3,2,1,0:T(8,128)(2,1)S(1)} async-done(((bf16[8,2,64,128]{3,2,1,0:T(8,128)(2,1)}), bf16[8,2,64,128]{3,2,1,0:T(8,128)(2,1)S(1)}, u32[]{:S(2)}, u32[]{:S(2)}) %all-to-all-start.1) | async-done | bytes 262176 | tf_op jit(solution)/shard_map/all_to_all | solution.py:343
  43.8 0.0 collective-permute-done.1.value_ref
  43.8 0.0 collective-permute-start.2
  43.8 0.1 pad_add_fusion.at_ref
  43.9 0.0 collective-permute-done.core_ref
  43.9 0.0 copy-done
  43.9 0.0 copy-done.1
  43.9 4.8 %first_half.1 = (f32[4,128,256]{2,1,0:T(8,128)S(1)}, f32[4,1,256]{2,1,0:T(1,128)S(1)}, f32[4,1,256]{2,1,0:T(1,128)S(1)}, f32[4,128,256]{2,1,0:T(8,128)S(1)}, f32...) custom-call(s32[2]{0:T(128)S(1)} %pad_add_fusion.at_ref, ...), custom_call_target="tpu_custom_call" | custom-call | flops 5000000000 | tf_op jit(solution)/shard_map/first_half/pallas_call | solution.py:310
  48.8 0.0 collective-permute-done.2.far_ref
  48.8 5.0 %second_half.1 = (bf16[8,2,64,128]{3,2,1,0:T(8,128)(2,1)S(1)}, f32[4,128,512]{2,1,0:T(8,128)S(1)}, f32[4,144,128]{2,1,0:T(8,128)S(1)}, bf16[4,144,256]{2,1,0:T(8,128)(2,1)S(1)}) custom-call(s32[2]{0:T(128)S(1)} %pad_add_fusion.at_ref, bf16[8,2,64,128]{3,2,1,0:T(8,128)(2,1)S(1)} %all-to-all-done.1.token_ref.rows_ref, bf16[8,2,64,256]{3,2,1,0:T(8,128)(2,1)S(1)} %tie.3.x_ref, ...), custom_call_target="tpu_custom_call" | custom-call | flops 5000000000 | tf_op jit(solution)/shard_map/second_half/pallas_call | solution.py:310
  53.7 4.4 %backward.1.one_ref = f32[2,64,128]{2,1,0:T(8,128)S(1)} custom-call(s32[2]{0:T(128)S(1)} %pad_add_fusion.at_ref, bf16[8,2,64,128]{3,2,1,0:T(8,128)(2,1)S(1)} %all-to-all-done.1.token_ref.rows_ref, bf16[8,2,64,256]{3,2,1,0:T(8,128)(2,1)S(1)} %all_to_all.15.token_ref.own_ref, bf16[8,2,64,256]{3,2,1,0:T(8,128)(2,1)S(1)} %collective-permute-done.core_ref, ...), custom_call_target="tpu_custom_call" | custom-call | flops 5000000000 | tf_op jit(solution)/shard_map/backward/pallas_call | solution.py:310
  58.2 0.6 collective-permute-start.3
  58.8 0.9 %collective-permute-done.3.two_ref = f32[2,64,128]{2,1,0:T(8,128)S(1)} collective-permute-done((f32[2,64,128]{2,1,0:T(8,128)S(1)}, f32[2,64,128]{2,1,0:T(8,128)S(1)}, u32[]{:S(2)}, u32[]{:S(2)}) %collective-permute-start.3) | collective-permute-done | bytes 65568 | tf_op jit(solution)/shard_map/ppermute | solution.py:340
  59.7 2.2 %collective-permute-start.6 = (bf16[2,64,128]{2,1,0:T(8,128)(2,1)S(1)}, bf16[2,64,128]{2,1,0:T(8,128)(2,1)S(1)}, u32[]{:S(2)}, u32[]{:S(2)}) collective-permute-start(bf16[2,64,128]{2,1,0:T(8,128)(2,1)S(1)} %pair.1.a_ref), channel_id=1, source_target_pairs={{0,136},{4,140},{8,128},{12,132},{16,152},{20,156},{24,144},{28,14... | collective-permute-start | bytes 98312 | tf_op jit(solution)/shard_map/ppermute | solution.py:409
  61.9 0.7 collective-permute-start.5
  62.6 1.3 %collective-permute-start.4 = (bf16[2,64,128]{2,1,0:T(8,128)(2,1)S(1)}, bf16[2,64,128]{2,1,0:T(8,128)(2,1)S(1)}, u32[]{:S(2)}, u32[]{:S(2)}) collective-permute-start(bf16[2,64,128]{2,1,0:T(8,128)(2,1)S(1)} %pair.1.a_ref), channel_id=1, source_target_pairs={{0,8},{4,12},{8,0},{12,4},{16,24},{20,28},{24,16},{28,20},{32,40},... | collective-permute-start | bytes 98312 | tf_op jit(solution)/shard_map/ppermute | solution.py:409
  63.9 1.0 %collective-permute-done.6.d_ref = bf16[2,64,128]{2,1,0:T(8,128)(2,1)S(1)} collective-permute-done((bf16[2,64,128]{2,1,0:T(8,128)(2,1)S(1)}, bf16[2,64,128]{2,1,0:T(8,128)(2,1)S(1)}, u32[]{:S(2)}, u32[]{:S(2)}) %collective-permute-start.6) | collective-permute-done | bytes 32800 | tf_op jit(solution)/shard_map/ppermute | solution.py:409
  64.9 2.7 %collective-permute-done.5.c_ref = bf16[2,64,128]{2,1,0:T(8,128)(2,1)S(1)} collective-permute-done((bf16[2,64,128]{2,1,0:T(8,128)(2,1)S(1)}, bf16[2,64,128]{2,1,0:T(8,128)(2,1)S(1)}, u32[]{:S(2)}, u32[]{:S(2)}) %collective-permute-start.5) | collective-permute-done | bytes 32800 | tf_op jit(solution)/shard_map/ppermute | solution.py:409
  67.6 0.0 collective-permute-done.4.b_ref
  67.6 0.1 share.1
  67.7 18.9 %all_to_all.16.whole_ref = bf16[8,2,64,256]{3,2,1,0:T(8,128)(2,1)S(1)} all-to-all(bf16[8,2,64,256]{3,2,1,0:T(8,128)(2,1)S(1)} %share.1), channel_id=1, replica_groups={{0,16,32,48,64,80,96,112},{4,20,36,52,68,84,100,116},{8,24,40,56,72,88,..., dimensions={0} | all-to-all | bytes 1048576 | tf_op jit(solution)/shard_map/all_to_all | solution.py:343
  86.6 1.4 %finish.1 = (bf16[1024,128]{1,0:T(8,128)(2,1)}, f32[8,64,128]{2,1,0:T(8,128)}, f32[8,64,128]{2,1,0:T(8,128)}) custom-call(s32[1]{0:T(128)} %get-tuple-element.20.flag_ref, bf16[8,2,64,256]{3,2,1,0:T(8,128)(2,1)S(1)} %all_to_all.16.whole_ref), custom_call_target="tpu_custom_call" | custom-call | tf_op jit(solution)/shard_map/finish/pallas_call | solution.py:420
  (3 shorter events, 0.0 us)
Async XLA Ops:
  28.5 15.3 %collective-permute-start.1 = (bf16[8,2,64,256]{3,2,1,0:T(8,128)(2,1)S(1)}, bf16[8,2,64,256]{3,2,1,0:T(8,128)(2,1)S(1)}, u32[]{:S(2)}, u32[]{:S(2)}) collective-permute-start(bf16[8,2,64,256]{3,2,1,0:T(8,128)(2,1)S(1)} %all_to_all.15.token_ref.own_ref), channel_id=1, source_target_pairs={{0,8},{4,12},{8,0},{12,4},{16,24},{20,28},{24,16},{28,20},{32,40},... | collective-permute-start | bytes 1572872 | tf_op jit(solution)/shard_map/ppermute | solution.py:340
  30.0 13.8 %all-to-all-start.1 = ((bf16[8,2,64,128]{3,2,1,0:T(8,128)(2,1)}), bf16[8,2,64,128]{3,2,1,0:T(8,128)(2,1)S(1)}, u32[]{:S(2)}, u32[]{:S(2)}) async-start(bf16[8,2,64,128]{3,2,1,0:T(8,128)(2,1)} %tie.2), calls=%async_computation.1 | async-start | bytes 524288 | tf_op jit(solution)/shard_map/all_to_all | solution.py:343
  33.4 10.5 %collective-permute-start = (bf16[8,2,64,256]{3,2,1,0:T(8,128)(2,1)S(1)}, bf16[8,2,64,256]{3,2,1,0:T(8,128)(2,1)S(1)}, u32[]{:S(2)}, u32[]{:S(2)}) collective-permute-start(bf16[8,2,64,256]{3,2,1,0:T(8,128)(2,1)S(1)} %all_to_all.15.token_ref.own_ref), channel_id=1, source_target_pairs={{0,4},{4,0},{8,12},{12,8},{16,20},{20,16},{24,28},{28,24},{32,36},... | collective-permute-start | bytes 1572872 | tf_op jit(solution)/shard_map/ppermute | solution.py:340
  33.6 10.4 %copy-start = (bf16[8,128,64]{1,2,0:T(8,128)(2,1)S(1)}, bf16[8,128,64]{1,2,0:T(8,128)(2,1)}, u32[]{:S(2)}) copy-start(bf16[8,128,64]{1,2,0:T(8,128)(2,1)} %param.10) | copy-start | bytes 393220
  33.6 10.4 %copy-start.1 = (bf16[8,128,64]{1,2,0:T(8,128)(2,1)S(1)}, bf16[8,128,64]{1,2,0:T(8,128)(2,1)}, u32[]{:S(2)}) copy-start(bf16[8,128,64]{1,2,0:T(8,128)(2,1)} %param.11) | copy-start | bytes 393220
  43.8 4.9 %collective-permute-start.2 = (bf16[8,2,64,256]{3,2,1,0:T(8,128)(2,1)S(1)}, bf16[8,2,64,256]{3,2,1,0:T(8,128)(2,1)S(1)}, u32[]{:S(2)}, u32[]{:S(2)}) collective-permute-start(bf16[8,2,64,256]{3,2,1,0:T(8,128)(2,1)S(1)} %tie.3.x_ref), channel_id=1, source_target_pairs={{0,4},{4,0},{8,12},{12,8},{16,20},{20,16},{24,28},{28,24},{32,36},... | collective-permute-start | bytes 1572872 | tf_op jit(solution)/shard_map/ppermute | solution.py:340
  58.2 1.5 %collective-permute-start.3 = (f32[2,64,128]{2,1,0:T(8,128)S(1)}, f32[2,64,128]{2,1,0:T(8,128)S(1)}, u32[]{:S(2)}, u32[]{:S(2)}) collective-permute-start(f32[2,64,128]{2,1,0:T(8,128)S(1)} %backward.1.one_ref), channel_id=1, source_target_pairs={{0,4},{4,0},{8,12},{12,8},{16,20},{20,16},{24,28},{28,24},{32,36},... | collective-permute-start | bytes 196616 | tf_op jit(solution)/shard_map/ppermute | solution.py:340
  59.7 5.2 %collective-permute-start.6 = (bf16[2,64,128]{2,1,0:T(8,128)(2,1)S(1)}, bf16[2,64,128]{2,1,0:T(8,128)(2,1)S(1)}, u32[]{:S(2)}, u32[]{:S(2)}) collective-permute-start(bf16[2,64,128]{2,1,0:T(8,128)(2,1)S(1)} %pair.1.a_ref), channel_id=1, source_target_pairs={{0,136},{4,140},{8,128},{12,132},{16,152},{20,156},{24,144},{28,14... | collective-permute-start | bytes 98312 | tf_op jit(solution)/shard_map/ppermute | solution.py:409
  61.9 5.7 %collective-permute-start.5 = (bf16[2,64,128]{2,1,0:T(8,128)(2,1)S(1)}, bf16[2,64,128]{2,1,0:T(8,128)(2,1)S(1)}, u32[]{:S(2)}, u32[]{:S(2)}) collective-permute-start(bf16[2,64,128]{2,1,0:T(8,128)(2,1)S(1)} %pair.1.a_ref), channel_id=1, source_target_pairs={{0,128},{4,132},{8,136},{12,140},{16,144},{20,148},{24,152},{28,15... | collective-permute-start | bytes 98312 | tf_op jit(solution)/shard_map/ppermute | solution.py:409
  62.6 5.0 %collective-permute-start.4 = (bf16[2,64,128]{2,1,0:T(8,128)(2,1)S(1)}, bf16[2,64,128]{2,1,0:T(8,128)(2,1)S(1)}, u32[]{:S(2)}, u32[]{:S(2)}) collective-permute-start(bf16[2,64,128]{2,1,0:T(8,128)(2,1)S(1)} %pair.1.a_ref), channel_id=1, source_target_pairs={{0,8},{4,12},{8,0},{12,4},{16,24},{20,28},{24,16},{28,20},{32,40},... | collective-permute-start | bytes 98312 | tf_op jit(solution)/shard_map/ppermute | solution.py:409

commit v3 on v2

--- a/solution.py
+++ b/solution.py
@@ -150,24 +150,17 @@
         keys.append(block_rows(refs, block, KEY))
         value = block_rows(refs, block, VALUE).T
         values_t.append(jnp.concatenate([value, jnp.ones((AUG - HD, HALF), BF16)], axis=0))
-    for block in range(BLOCKS):
-        phi = features(dot(wk, keys[block], NT))
-        phik_ref[block] = phi
-        phi16 = phi.astype(BF16)
-        state_ref[block] = dot(values_t[block], phi16, NT)
-        pair = dot(phi16.T, phi_q[block])
-        pair = jnp.where(masks[block // 2], pair, 0.0)
-        if block == 0:
-            high, low = split(pair)
-            num_ref[block] = dot(values_t[block], high) + dot(values_t[block], low)
-        else:
-            num_ref[block] = dot(values_t[block], pair.astype(BF16))
-
+    def scores_of(block):
         scores = [dot(keys[b], queries[block], NT) for b in range(block + 1)]
         scores[-1] = jnp.where(masks[block // 2], scores[-1], -1e30)
         top = jnp.max(scores[0], axis=0, keepdims=True)
         for s in scores[1:]:
             top = jnp.maximum(top, jnp.max(s, axis=0, keepdims=True))
+        return scores, top
+
+    ready = [scores_of(block) for block in range(BLOCKS)]
+    for block in range(BLOCKS):
+        scores, top = ready[block]
         total, acc = 0.0, 0.0
         for b, s in enumerate(scores):
             weights = jnp.exp2(s * scale - top * scale)
@@ -176,6 +169,17 @@
         top_ref[block] = top * scale
         total_ref[block] = total
         acc_ref[block] = acc
+    phis = [features(dot(wk, keys[b], NT)) for b in range(BLOCKS)]
+    phi16s = [phi.astype(BF16) for phi in phis]
+    pairs = [dot(phi16s[b], phi_q[b], (((0,), (0,)), ((), ()))) for b in range(BLOCKS)]
+    for b in range(BLOCKS):
+        phik_ref[b] = phis[b]
+        state_ref[b] = dot(values_t[b], phi16s[b], NT)
+    pairs = [jnp.where(masks[b // 2], pairs[b], 0.0) for b in range(BLOCKS)]
+    high, low = split(pairs[0])
+    num_ref[0] = dot(values_t[0], high) + dot(values_t[0], low)
+    for b in range(1, BLOCKS):
+        num_ref[b] = dot(values_t[b], pairs[b].astype(BF16))
 
 
 def first_kernel(at_ref, rows_ref, own_ref, core_ref, wq_ref, wk_ref, phiq_ref, *outs):
@@ -202,31 +206,39 @@
     phi_q = [phiq_ref[block].astype(BF16) for block in range(BLOCKS)]
     outs = (top2_ref, total2_ref, acc2_ref, num2_ref, state2_ref, phik_ref)
     half_forward((x_ref, far_ref), masks, queries, phi_q, wk_ref[place], outs)
-    prior = jnp.zeros((AUG, PHI), F32)
-    for block in range(BLOCKS):
-        top = jnp.maximum(top_ref[block], top2_ref[block])
-        one = jnp.exp2(top_ref[block] - top)
-        two = jnp.exp2(top2_ref[block] - top)
-        total = total_ref[block] * one + total2_ref[block] * two
-        teacher = (acc_ref[block] * one + acc2_ref[block] * two) * (1.0 / total)
-        prior_ref[block] = prior
-        numerator = num_ref[block] + num2_ref[block]
-        if block > 0:
-            numerator = numerator + dot(prior.astype(BF16), phi_q[block])
-        prior = prior + state_ref[block] + state2_ref[block]
-        inverse = 1.0 / numerator[HD:HD + 1]
-        y = numerator[:HD] * inverse
-        d_num = (y - teacher) * (inverse * LOSS)
-        d_den = -jnp.sum(d_num * y, axis=0, keepdims=True)
+    span = range(BLOCKS)
+    priors = [None] * BLOCKS
+    prior = state_ref[0] + state2_ref[0]
+    prior_ref[0] = jnp.zeros((AUG, PHI), F32)
+    for b in range(1, BLOCKS):
+        priors[b] = prior
+        prior_ref[b] = prior
+        prior = prior + state_ref[b] + state2_ref[b]
+    numerators = [num_ref[b] + num2_ref[b] for b in span]
+    for b in range(1, BLOCKS):
+        numerators[b] = numerators[b] + dot(priors[b].astype(BF16), phi_q[b])
+    teachers = []
+    for b in span:
+        top = jnp.maximum(top_ref[b], top2_ref[b])
+        one = jnp.exp2(top_ref[b] - top)
+        two = jnp.exp2(top2_ref[b] - top)
+        total = total_ref[b] * one + total2_ref[b] * two
+        teachers.append((acc_ref[b] * one + acc2_ref[b] * two) * (1.0 / total))
+    inverses = [1.0 / numerators[b][HD:HD + 1] for b in span]
+    ys = [numerators[b][:HD] * inverses[b] for b in span]
+    index = lax.broadcasted_iota(jnp.int32, (AUG - HD, ROWS), 0)
+    for b in span:
+        d_num = (ys[b] - teachers[b]) * (inverses[b] * LOSS)
+        d_den = -jnp.sum(d_num * ys[b], axis=0, keepdims=True)
         den_high, den_low = split(d_den)
-        index = lax.broadcasted_iota(jnp.int32, (AUG - HD, ROWS), 0)
         extra = jnp.where(
             index == 0, den_high.astype(F32), jnp.where(index == 1, den_low.astype(F32), 0.0)
         )
-        dn_ref[block] = jnp.concatenate([d_num.astype(BF16), extra.astype(BF16)], axis=0)
-        rows = y.T.astype(BF16)
+        dn_ref[b] = jnp.concatenate([d_num.astype(BF16), extra.astype(BF16)], axis=0)
+    for b in span:
+        rows = ys[b].astype(BF16).T
         for i in range(4):
-            place, late = where_is(4 * block + i)
+            place, late = where_is(4 * b + i)
             student_ref[place, late] = rows[i * SEG:(i + 1) * SEG]
 
 
@@ -253,43 +265,72 @@
         product = dot(jnp.concatenate(split(back), axis=0), rows)
         return product[:FD] + product[FD:]
 
-    grad_q = jnp.zeros((FD, HD), F32)
-    grad_k = jnp.zeros((FD, HD), F32)
-    later = jnp.zeros((PHI, AUG), F32)
-    for block in reversed(range(BLOCKS)):
-        first = block == 0
-        values = both(block, VALUE)
-        keys = both(block, KEY)
-        queries = block_rows((rows_ref,), block, QUERY)
-        phi_q = phiq_ref[block]
-        phi_q16 = phi_q.astype(BF16)
-        phi_k = jnp.concatenate([phik_ref[block], phik2_ref[block]], axis=1)
-        grads = dn_ref[block]
-        d_den = grads[HD:HD + 1].astype(F32) + grads[HD + 1:HD + 2].astype(F32)
-        pair = dot(values, grads[:HD]) + d_den
-        pair = jnp.where(masks[block // 2], pair, 0.0).astype(BF16)
-        if first:
-            grad_phi = dot(jnp.concatenate(split(phi_k), axis=0), pair)
-            grad_phi = grad_phi[:PHI] + grad_phi[PHI:]
+    span = range(BLOCKS)
+    values = [both(b, VALUE) for b in span]
+    keys = [both(b, KEY) for b in span]
+    queries = [block_rows((rows_ref,), b, QUERY) for b in span]
+    phi_q = [phiq_ref[b] for b in span]
+    phi_q16 = [p.astype(BF16) for p in phi_q]
+    phi_k = [jnp.concatenate([phik_ref[b], phik2_ref[b]], axis=1) for b in span]
+    grads = [dn_ref[b] for b in span]
+    pairs = []
+    for b in span:
+        d_den = grads[b][HD:HD + 1].astype(F32) + grads[b][HD + 1:HD + 2].astype(F32)
+        pair = dot(values[b], grads[b][:HD]) + d_den
+        pairs.append(jnp.where(masks[b // 2], pair, 0.0).astype(BF16))
+    terms = [dot(phi_q16[b], grads[b], NT) if b > 0 else None for b in span]
+    later = [None] * BLOCKS
+    total = terms[3]
+    for b in (2, 1, 0):
+        later[b] = total
+        if b > 0:
+            total = total + terms[b]
+    grad_phi_q = []
+    for b in span:
+        if b == 0:
+            both_terms = dot(jnp.concatenate(split(phi_k[b]), axis=0), pairs[b])
+            grad_phi_q.append(both_terms[:PHI] + both_terms[PHI:])
         else:
-            prior = prior_ref[block].T
-            grad_phi = dot(phi_k.astype(BF16), pair) + dot(prior.astype(BF16), grads)
-        grad_q = grad_q + project(phi_q, grad_phi, queries, first)
-
-        if block == BLOCKS - 1:
-            grad_phi = dot(phi_q16, pair, NT)
+            prior = prior_ref[b].T
+            grad_phi_q.append(
+                dot(phi_k[b].astype(BF16), pairs[b]) + dot(prior.astype(BF16), grads[b])
+            )
+    grad_phi_k = []
+    for b in span:
+        if b == BLOCKS - 1:
+            grad_phi_k.append(dot(phi_q16[b], pairs[b], NT))
         else:
-            grad_phi = dot(
-                jnp.concatenate([phi_q16, later[:, :HD].astype(BF16)], axis=1),
-                jnp.concatenate([pair, values], axis=1),
+            grad = dot(
+                jnp.concatenate([phi_q16[b], later[b][:, :HD].astype(BF16)], axis=1),
+                jnp.concatenate([pairs[b], values[b]], axis=1),
                 NT,
             )
-            grad_phi = grad_phi + (later[:, HD:HD + 1] + later[:, HD + 1:HD + 2])
-        grad_k = grad_k + project(phi_k, grad_phi, keys, first)
-        if not first:
-            later = later + dot(phi_q16, grads, NT)
+            grad_phi_k.append(grad + (later[b][:, HD:HD + 1] + later[b][:, HD + 1:HD + 2]))
+    grad_q = project(phi_q[0], grad_phi_q[0], queries[0], True)
+    for b in range(1, BLOCKS):
+        grad_q = grad_q + project(phi_q[b], grad_phi_q[b], queries[b], False)
+    grad_k = project(phi_k[0], grad_phi_k[0], keys[0], True)
+    for b in range(1, BLOCKS):
+        grad_k = grad_k + project(phi_k[b], grad_phi_k[b], keys[b], False)
     grad_ref[0] = grad_q.astype(grad_ref.dtype)
     grad_ref[1] = grad_k.astype(grad_ref.dtype)
+
+
+def rest_kernel(
+    at_ref, rows_ref, own_ref, core_ref, x_ref, far_ref, wk_ref, phiq_ref,
+    top_ref, total_ref, acc_ref, num_ref, state_ref, phik_ref,
+    student_ref, grad_ref,
+    phik2_ref, prior_ref, dn_ref, *partial,
+):
+    second_kernel(
+        at_ref, rows_ref, x_ref, far_ref, wk_ref, phiq_ref,
+        top_ref, total_ref, acc_ref, num_ref, state_ref,
+        student_ref, phik2_ref, prior_ref, dn_ref, *partial,
+    )
+    backward_kernel(
+        at_ref, rows_ref, own_ref, core_ref, x_ref, far_ref, phiq_ref, phik_ref, phik2_ref,
+        prior_ref, dn_ref, grad_ref,
+    )
 
 
 VMEM = pl.BlockSpec(memory_space=pltpu.VMEM)
@@ -385,25 +426,13 @@
     )
     beside = tied(beside, rows)
     far = swap(beside, 1)
-    student, phi_k2, prior, grads = call(
-        second_kernel, "second_half",
-        [
-            ((PLACES, 2, SEG, HD), BF16),
-            PHI_KEYS,
-            ((BLOCKS, AUG, PHI), F32),
-            ((BLOCKS, AUG, ROWS), BF16),
-        ],
-        (at, rows, beside, far, wk, phi_q, *first[:5]),
-        PARTIAL,
-        flops=5 * 10 ** 9,
-    )
-    (grad,) = call(
-        backward_kernel, "backward",
-        [((2, FD, HD), F32)],
-        (at, rows, own, core, beside, far, phi_q, first[5], phi_k2, prior, grads),
-        flops=5 * 10 ** 9,
-    )
-
+    student, grad = call(
+        rest_kernel, "rest",
+        [((PLACES, 2, SEG, HD), BF16), ((2, FD, HD), F32)],
+        (at, rows, own, core, beside, far, wk, phi_q, *first),
+        [PHI_KEYS, ((BLOCKS, AUG, PHI), F32), ((BLOCKS, AUG, ROWS), BF16)] + PARTIAL,
+        flops=10 ** 10,
+    )
     def swap_wide(array, relative):
         pairs = [(i, i ^ relative) for i in range(64)]
         return lax.ppermute(array, ("dp", "ctx"), pairs)

time: 88.4 us -> 83.8 us (0.948)
  Pallas kernels: 17.6 us -> 13 us
    pallas_call x5 -> x4, Pallas kernels: 14.3 us -> 9.68 us  [call(): pl.pallas_call(kernel, out_shape=[jax.ShapeDtypeStruct(*out) for out in o...]
  transfers between devices with their start and end apart: 8 -> 8, of which waited for: 4 -> 4; matrix products, arithmetic and copies ran while one was open for 0% -> 0% of each run, Pallas kernels for 5% -> 4%
where the time goes in v3:
time: 83.8 us; the launch traced here: 83.4 us
  blocking collectives  44.9 us (54%)
  waiting for transfers between devices  14.9 us (18%)
  Pallas kernels  13 us (16%)
  starting transfers between devices  9.76 us (12%)
    all_to_all x2, blocking collectives, along_z(): return lax.all_to_all(array, 'ctx', 0, 0, axis_index_groups=z_groups)  44.9 us
    all_to_all x1, waiting for transfers between devices, along_z(): return lax.all_to_all(array, 'ctx', 0, 0, axis_index_groups=z_groups)  10.3 us
    pallas_call x4, Pallas kernels, call(): pl.pallas_call(kernel, out_shape=[jax.ShapeDtypeStruct(*out) for out in o...  9.68 us
    ppermute x3, starting transfers between devices, swap_wide(): return lax.ppermute(array, ('dp', 'ctx'), pairs)  4.18 us
    ppermute x3, waiting for transfers between devices, swap_wide(): return lax.ppermute(array, ('dp', 'ctx'), pairs)  3.74 us
    all_to_all x1, starting transfers between devices, along_z(): return lax.all_to_all(array, 'ctx', 0, 0, axis_index_groups=z_groups)  3.41 us
    ppermute x4, starting transfers between devices, swap(): return lax.ppermute(array, 'ctx', [(i, i ^ relative) for i in range(32)])  2.17 us
    pallas_call x1, Pallas kernels, on_device(): pl.pallas_call(pack_kernel, out_shape=[jax.ShapeDtypeStruct((PLACES, 2, S...  1.91 us
  transfers between devices with their start and end apart: 8, of which 4 were waited for; matrix products, arithmetic and copies ran while one was open for 0% of the time, Pallas kernels for 4%

profile of v3, /device:TPU:16, one launch (start us, length us, event | category | flops | bytes accessed | tf_op | source)
XLA Modules:
  0.0 83.4 jit_solution(18441714218056670760)
XLA Ops:
  0.6 1.9 %pack.1 = (bf16[8,2,64,256]{3,2,1,0:T(8,128)(2,1)}, bf16[8,2,64,128]{3,2,1,0:T(8,128)(2,1)}, s32[1]{0:T(128)}) custom-call(s32[2]{0:T(128)} %ids_ref.1, bf16[1024,128]{1,0:T(8,128)(2,1)} %bitcast.15, bf16[128,128]{1,0:T(8,128)(2,1)} %bitcast.16, bf16[128,128]{1,0:T(8,128)(2,1)} %bitcast.17), custom_call_target="tpu_custom_call" | custom-call | tf_op jit(solution)/shard_map/pack/pallas_call | solution.py:388
  2.5 26.0 %all_to_all.15.token_ref.own_ref = bf16[8,2,64,256]{3,2,1,0:T(8,128)(2,1)S(1)} all-to-all(bf16[8,2,64,256]{3,2,1,0:T(8,128)(2,1)} %get-tuple-element.20), channel_id=1, replica_groups={{0,16,32,48,64,80,96,112},{4,20,36,52,68,84,100,116},{8,24,40,56,72,88,..., dimensions={0} | all-to-all | bytes 1048576 | tf_op jit(solution)/shard_map/all_to_all | solution.py:384
  28.5 1.5 %collective-permute-start.1 = (bf16[8,2,64,256]{3,2,1,0:T(8,128)(2,1)S(1)}, bf16[8,2,64,256]{3,2,1,0:T(8,128)(2,1)S(1)}, u32[]{:S(2)}, u32[]{:S(2)}) collective-permute-start(bf16[8,2,64,256]{3,2,1,0:T(8,128)(2,1)S(1)} %all_to_all.15.token_ref.own_ref), channel_id=1, source_target_pairs={{0,8},{4,12},{8,0},{12,4},{16,24},{20,28},{24,16},{28,20},{32,40},... | collective-permute-start | bytes 1572872 | tf_op jit(solution)/shard_map/ppermute | solution.py:381
  30.0 3.4 %all-to-all-start.1 = ((bf16[8,2,64,128]{3,2,1,0:T(8,128)(2,1)}), bf16[8,2,64,128]{3,2,1,0:T(8,128)(2,1)S(1)}, u32[]{:S(2)}, u32[]{:S(2)}) async-start(bf16[8,2,64,128]{3,2,1,0:T(8,128)(2,1)} %tie.2), calls=%async_computation.1 | async-start | bytes 524288 | tf_op jit(solution)/shard_map/all_to_all | solution.py:384
  33.4 0.1 collective-permute-start
  33.6 0.0 copy-start
  33.6 0.0 copy-start.1
  33.6 10.3 %all-to-all-done.1.token_ref.rows_ref = bf16[8,2,64,128]{3,2,1,0:T(8,128)(2,1)S(1)} async-done(((bf16[8,2,64,128]{3,2,1,0:T(8,128)(2,1)}), bf16[8,2,64,128]{3,2,1,0:T(8,128)(2,1)S(1)}, u32[]{:S(2)}, u32[]{:S(2)}) %all-to-all-start.1) | async-done | bytes 262176 | tf_op jit(solution)/shard_map/all_to_all | solution.py:384
  43.8 0.0 collective-permute-done.1.value_ref
  43.8 0.0 collective-permute-start.2
  43.8 0.1 pad_add_fusion.at_ref
  43.9 0.0 collective-permute-done.core_ref
  43.9 0.0 copy-done
  43.9 0.0 copy-done.1
  43.9 3.5 %first_half.1 = (f32[4,128,256]{2,1,0:T(8,128)S(1)}, f32[4,1,256]{2,1,0:T(1,128)S(1)}, f32[4,1,256]{2,1,0:T(1,128)S(1)}, f32[4,128,256]{2,1,0:T(8,128)S(1)}, f32...) custom-call(s32[2]{0:T(128)S(1)} %pad_add_fusion.at_ref, ...), custom_call_target="tpu_custom_call" | custom-call | flops 5000000000 | tf_op jit(solution)/shard_map/first_half/pallas_call | solution.py:351
  47.5 0.0 collective-permute-done.2.far_ref
  47.5 6.1 %rest.1 = (bf16[8,2,64,128]{3,2,1,0:T(8,128)(2,1)S(1)}, f32[2,64,128]{2,1,0:T(8,128)S(1)}) custom-call(s32[2]{0:T(128)S(1)} %pad_add_fusion.at_ref, bf16[8,2,64,128]{3,2,1,0:T(8,128)(2,1)S(1)} %all-to-all-done.1.token_ref.rows_ref, bf16[8,2,64,256]{3,2,1,0:T(8,128)(2,1)S(1)} %all_to_all.15.token_ref.own_ref, ...), custom_call_target="tpu_custom_call" | custom-call | flops 10000000000 | tf_op jit(solution)/shard_map/rest/pallas_call | solution.py:351
  53.5 0.6 collective-permute-start.3
  54.1 0.9 %collective-permute-done.3.two_ref = f32[2,64,128]{2,1,0:T(8,128)S(1)} collective-permute-done((f32[2,64,128]{2,1,0:T(8,128)S(1)}, f32[2,64,128]{2,1,0:T(8,128)S(1)}, u32[]{:S(2)}, u32[]{:S(2)}) %collective-permute-start.3) | collective-permute-done | bytes 65568 | tf_op jit(solution)/shard_map/ppermute | solution.py:381
  55.0 2.2 %collective-permute-start.6 = (bf16[2,64,128]{2,1,0:T(8,128)(2,1)S(1)}, bf16[2,64,128]{2,1,0:T(8,128)(2,1)S(1)}, u32[]{:S(2)}, u32[]{:S(2)}) collective-permute-start(bf16[2,64,128]{2,1,0:T(8,128)(2,1)S(1)} %pair.1.a_ref), channel_id=1, source_target_pairs={{0,136},{4,140},{8,128},{12,132},{16,152},{20,156},{24,144},{28,14... | collective-permute-start | bytes 98312 | tf_op jit(solution)/shard_map/ppermute | solution.py:438
  57.2 0.7 collective-permute-start.5
  58.0 1.3 %collective-permute-start.4 = (bf16[2,64,128]{2,1,0:T(8,128)(2,1)S(1)}, bf16[2,64,128]{2,1,0:T(8,128)(2,1)S(1)}, u32[]{:S(2)}, u32[]{:S(2)}) collective-permute-start(bf16[2,64,128]{2,1,0:T(8,128)(2,1)S(1)} %pair.1.a_ref), channel_id=1, source_target_pairs={{0,8},{4,12},{8,0},{12,4},{16,24},{20,28},{24,16},{28,20},{32,40},... | collective-permute-start | bytes 98312 | tf_op jit(solution)/shard_map/ppermute | solution.py:438
  59.2 1.0 %collective-permute-done.6.d_ref = bf16[2,64,128]{2,1,0:T(8,128)(2,1)S(1)} collective-permute-done((bf16[2,64,128]{2,1,0:T(8,128)(2,1)S(1)}, bf16[2,64,128]{2,1,0:T(8,128)(2,1)S(1)}, u32[]{:S(2)}, u32[]{:S(2)}) %collective-permute-start.6) | collective-permute-done | bytes 32800 | tf_op jit(solution)/shard_map/ppermute | solution.py:438
  60.3 2.7 %collective-permute-done.5.c_ref = bf16[2,64,128]{2,1,0:T(8,128)(2,1)S(1)} collective-permute-done((bf16[2,64,128]{2,1,0:T(8,128)(2,1)S(1)}, bf16[2,64,128]{2,1,0:T(8,128)(2,1)S(1)}, u32[]{:S(2)}, u32[]{:S(2)}) %collective-permute-start.5) | collective-permute-done | bytes 32800 | tf_op jit(solution)/shard_map/ppermute | solution.py:438
  63.0 0.0 collective-permute-done.4.b_ref
  63.0 0.1 share.1
  63.1 18.9 %all_to_all.16.whole_ref = bf16[8,2,64,256]{3,2,1,0:T(8,128)(2,1)S(1)} all-to-all(bf16[8,2,64,256]{3,2,1,0:T(8,128)(2,1)S(1)} %share.1), channel_id=1, replica_groups={{0,16,32,48,64,80,96,112},{4,20,36,52,68,84,100,116},{8,24,40,56,72,88,..., dimensions={0} | all-to-all | bytes 1048576 | tf_op jit(solution)/shard_map/all_to_all | solution.py:384
  82.0 1.4 %finish.1 = (bf16[1024,128]{1,0:T(8,128)(2,1)}, f32[8,64,128]{2,1,0:T(8,128)}, f32[8,64,128]{2,1,0:T(8,128)}) custom-call(s32[1]{0:T(128)} %get-tuple-element.18.flag_ref, bf16[8,2,64,256]{3,2,1,0:T(8,128)(2,1)S(1)} %all_to_all.16.whole_ref), custom_call_target="tpu_custom_call" | custom-call | tf_op jit(solution)/shard_map/finish/pallas_call | solution.py:449
  (3 shorter events, 0.0 us)
Async XLA Ops:
  28.5 15.3 %collective-permute-start.1 = (bf16[8,2,64,256]{3,2,1,0:T(8,128)(2,1)S(1)}, bf16[8,2,64,256]{3,2,1,0:T(8,128)(2,1)S(1)}, u32[]{:S(2)}, u32[]{:S(2)}) collective-permute-start(bf16[8,2,64,256]{3,2,1,0:T(8,128)(2,1)S(1)} %all_to_all.15.token_ref.own_ref), channel_id=1, source_target_pairs={{0,8},{4,12},{8,0},{12,4},{16,24},{20,28},{24,16},{28,20},{32,40},... | collective-permute-start | bytes 1572872 | tf_op jit(solution)/shard_map/ppermute | solution.py:381
  30.0 13.8 %all-to-all-start.1 = ((bf16[8,2,64,128]{3,2,1,0:T(8,128)(2,1)}), bf16[8,2,64,128]{3,2,1,0:T(8,128)(2,1)S(1)}, u32[]{:S(2)}, u32[]{:S(2)}) async-start(bf16[8,2,64,128]{3,2,1,0:T(8,128)(2,1)} %tie.2), calls=%async_computation.1 | async-start | bytes 524288 | tf_op jit(solution)/shard_map/all_to_all | solution.py:384
  33.4 10.5 %collective-permute-start = (bf16[8,2,64,256]{3,2,1,0:T(8,128)(2,1)S(1)}, bf16[8,2,64,256]{3,2,1,0:T(8,128)(2,1)S(1)}, u32[]{:S(2)}, u32[]{:S(2)}) collective-permute-start(bf16[8,2,64,256]{3,2,1,0:T(8,128)(2,1)S(1)} %all_to_all.15.token_ref.own_ref), channel_id=1, source_target_pairs={{0,4},{4,0},{8,12},{12,8},{16,20},{20,16},{24,28},{28,24},{32,36},... | collective-permute-start | bytes 1572872 | tf_op jit(solution)/shard_map/ppermute | solution.py:381
  33.6 10.4 %copy-start = (bf16[8,128,64]{1,2,0:T(8,128)(2,1)S(1)}, bf16[8,128,64]{1,2,0:T(8,128)(2,1)}, u32[]{:S(2)}) copy-start(bf16[8,128,64]{1,2,0:T(8,128)(2,1)} %param.10) | copy-start | bytes 393220
  33.6 10.4 %copy-start.1 = (bf16[8,128,64]{1,2,0:T(8,128)(2,1)S(1)}, bf16[8,128,64]{1,2,0:T(8,128)(2,1)}, u32[]{:S(2)}) copy-start(bf16[8,128,64]{1,2,0:T(8,128)(2,1)} %param.11) | copy-start | bytes 393220
  43.8 3.6 %collective-permute-start.2 = (bf16[8,2,64,256]{3,2,1,0:T(8,128)(2,1)S(1)}, bf16[8,2,64,256]{3,2,1,0:T(8,128)(2,1)S(1)}, u32[]{:S(2)}, u32[]{:S(2)}) collective-permute-start(bf16[8,2,64,256]{3,2,1,0:T(8,128)(2,1)S(1)} %tie.3.x_ref), channel_id=1, source_target_pairs={{0,4},{4,0},{8,12},{12,8},{16,20},{20,16},{24,28},{28,24},{32,36},... | collective-permute-start | bytes 1572872 | tf_op jit(solution)/shard_map/ppermute | solution.py:381
  53.5 1.5 %collective-permute-start.3 = (f32[2,64,128]{2,1,0:T(8,128)S(1)}, f32[2,64,128]{2,1,0:T(8,128)S(1)}, u32[]{:S(2)}, u32[]{:S(2)}) collective-permute-start(f32[2,64,128]{2,1,0:T(8,128)S(1)} %get-tuple-element.28.one_ref), channel_id=1, source_target_pairs={{0,4},{4,0},{8,12},{12,8},{16,20},{20,16},{24,28},{28,24},{32,36},... | collective-permute-start | bytes 196616 | tf_op jit(solution)/shard_map/ppermute | solution.py:381
  55.0 5.2 %collective-permute-start.6 = (bf16[2,64,128]{2,1,0:T(8,128)(2,1)S(1)}, bf16[2,64,128]{2,1,0:T(8,128)(2,1)S(1)}, u32[]{:S(2)}, u32[]{:S(2)}) collective-permute-start(bf16[2,64,128]{2,1,0:T(8,128)(2,1)S(1)} %pair.1.a_ref), channel_id=1, source_target_pairs={{0,136},{4,140},{8,128},{12,132},{16,152},{20,156},{24,144},{28,14... | collective-permute-start | bytes 98312 | tf_op jit(solution)/shard_map/ppermute | solution.py:438
  57.2 5.7 %collective-permute-start.5 = (bf16[2,64,128]{2,1,0:T(8,128)(2,1)S(1)}, bf16[2,64,128]{2,1,0:T(8,128)(2,1)S(1)}, u32[]{:S(2)}, u32[]{:S(2)}) collective-permute-start(bf16[2,64,128]{2,1,0:T(8,128)(2,1)S(1)} %pair.1.a_ref), channel_id=1, source_target_pairs={{0,128},{4,132},{8,136},{12,140},{16,144},{20,148},{24,152},{28,15... | collective-permute-start | bytes 98312 | tf_op jit(solution)/shard_map/ppermute | solution.py:438
  58.0 5.0 %collective-permute-start.4 = (bf16[2,64,128]{2,1,0:T(8,128)(2,1)S(1)}, bf16[2,64,128]{2,1,0:T(8,128)(2,1)S(1)}, u32[]{:S(2)}, u32[]{:S(2)}) collective-permute-start(bf16[2,64,128]{2,1,0:T(8,128)(2,1)S(1)} %pair.1.a_ref), channel_id=1, source_target_pairs={{0,8},{4,12},{8,0},{12,4},{16,24},{20,28},{24,16},{28,20},{32,40},... | collective-permute-start | bytes 98312 | tf_op jit(solution)/shard_map/ppermute | solution.py:438

commit v4 on v3

--- a/solution.py
+++ b/solution.py
@@ -18,6 +18,7 @@
 HALF = 8 * SEG
 AUG = HD + 16
 LOSS = 1.0 / 8192.0
+SCALE = (HD ** -0.5) * math.log2(math.e)
 F32 = jnp.float32
 BF16 = jnp.bfloat16
 NN = (((1,), (0,)), ((), ()))
@@ -125,26 +126,32 @@
     two = c_ref[...].astype(F32) + d_ref[...].astype(F32)
     total = (one + two).astype(BF16)
     for place in range(PLACES):
-        out_ref[place, :, :, :HD] = student_ref[place]
-        out_ref[place, :, :, HD:] = total
-
-
-def finish_kernel(flag_ref, whole_ref, student_ref, gq_ref, gk_ref, wide):
-    for place in range(PLACES):
-        gq_ref[place] = whole_ref[place, 0, :, HD:].astype(F32)
-        gk_ref[place] = whole_ref[place, 1, :, HD:].astype(F32)
+        out_ref[place, :2] = student_ref[place]
+        out_ref[place, 2] = total
+
+
+def student_kernel(flag_ref, whole_ref, student_ref, wide):
     swapped = flag_ref[0] == 1
     for late in range(2):
         start = pl.multiple_of(jnp.where(swapped, SEG - SEG * late, SEG * late), SEG)
         for place in range(PLACES):
             rows = pl.ds(start * PLACES + place, SEG, stride=PLACES)
-            wide[rows] = whole_ref[place, late, :, :HD].astype(F32)
+            wide[rows] = whole_ref[place, late].astype(F32)
     student_ref[...] = wide[...].astype(BF16)
+
+
+def finish_kernel(at_ref, rows_ref, whole_ref, other_ref, student_ref, gq_ref, gk_ref):
+    odd = at_ref[1] % 2 == 1
+    student_ref[...] = rows_ref[...]
+    for place in range(PLACES):
+        mine = whole_ref[place, 2].astype(F32)
+        other = other_ref[place].astype(F32)
+        gq_ref[place] = jnp.where(odd, other, mine)
+        gk_ref[place] = jnp.where(odd, mine, other)
 
 
 def half_forward(refs, masks, queries, phi_q, wk, outs):
     top_ref, total_ref, acc_ref, num_ref, state_ref, phik_ref = outs
-    scale = (HD ** -0.5) * math.log2(math.e)
     keys, values_t = [], []
     for block in range(BLOCKS):
         keys.append(block_rows(refs, block, KEY))
@@ -163,10 +170,10 @@
         scores, top = ready[block]
         total, acc = 0.0, 0.0
         for b, s in enumerate(scores):
-            weights = jnp.exp2(s * scale - top * scale)
+            weights = jnp.exp2((s - top) * SCALE)
             total = total + jnp.sum(weights, axis=0, keepdims=True)
             acc = acc + dot(values_t[b][:HD], weights.astype(BF16))
-        top_ref[block] = top * scale
+        top_ref[block] = top
         total_ref[block] = total
         acc_ref[block] = acc
     phis = [features(dot(wk, keys[b], NT)) for b in range(BLOCKS)]
@@ -220,8 +227,8 @@
     teachers = []
     for b in span:
         top = jnp.maximum(top_ref[b], top2_ref[b])
-        one = jnp.exp2(top_ref[b] - top)
-        two = jnp.exp2(top2_ref[b] - top)
+        one = jnp.exp2((top_ref[b] - top) * SCALE)
+        two = jnp.exp2((top2_ref[b] - top) * SCALE)
         total = total_ref[b] * one + total2_ref[b] * two
         teachers.append((acc_ref[b] * one + acc2_ref[b] * two) * (1.0 / total))
     inverses = [1.0 / numerators[b][HD:HD + 1] for b in span]
@@ -312,8 +319,9 @@
     grad_k = project(phi_k[0], grad_phi_k[0], keys[0], True)
     for b in range(1, BLOCKS):
         grad_k = grad_k + project(phi_k[b], grad_phi_k[b], keys[b], False)
-    grad_ref[0] = grad_q.astype(grad_ref.dtype)
-    grad_ref[1] = grad_k.astype(grad_ref.dtype)
+    odd = at_ref[1] % 2 == 1
+    grad_ref[0] = jnp.where(odd, grad_k, grad_q)
+    grad_ref[1] = jnp.where(odd, grad_q, grad_k)
 
 
 def rest_kernel(
@@ -438,27 +446,24 @@
         return lax.ppermute(array, ("dp", "ctx"), pairs)
 
     (pair,) = call(
-        pair_kernel, "pair", [((2, FD, HD), BF16)], (grad, swap(grad, 1)), smem=False
+        pair_kernel, "pair", [((FD, HD), BF16)], (grad[0], swap(grad[1], 1)), smem=False
     )
     (share,) = call(
-        share_kernel, "share", [((PLACES, 2, SEG, 2 * HD), BF16)],
+        share_kernel, "share", [((PLACES, 3, SEG, HD), BF16)],
         (pair, swap_wide(pair, 2), swap_wide(pair, 32), swap_wide(pair, 34), student),
         smem=False,
     )
     whole = along_z(share)
-    student, grad_query, grad_key = pl.pallas_call(
-        finish_kernel,
-        out_shape=[
-            jax.ShapeDtypeStruct((2 * SEG * PLACES, HD), BF16),
-            jax.ShapeDtypeStruct((PLACES, FD, HD), F32),
-            jax.ShapeDtypeStruct((PLACES, FD, HD), F32),
-        ],
-        in_specs=[SMEM, VMEM],
-        out_specs=[VMEM] * 3,
-        scratch_shapes=[pltpu.VMEM((2 * SEG * PLACES, HD), F32)],
-        compiler_params=PARAMS,
-        name="finish",
-    )(flag, whole)
+    other = swap(whole[:, 2], 1)
+    (student,) = call(
+        student_kernel, "student_rows", [((2 * SEG * PLACES, HD), BF16)], (flag, whole),
+        [((2 * SEG * PLACES, HD), F32)],
+    )
+    student, grad_query, grad_key = call(
+        finish_kernel, "finish",
+        [((2 * SEG * PLACES, HD), BF16)] + [((PLACES, FD, HD), F32)] * 2,
+        (at, student, whole, other),
+    )
     student = student.reshape(2 * SEG, 1, PLACES, HD)
     return student, jnp.transpose(grad_query, (0, 2, 1)), jnp.transpose(grad_key, (0, 2, 1))
 

time: 83.8 us -> 83.1 us (level); the launches traced: 83.4 us -> 81.6 us
  blocking collectives: 44.9 us -> 42.2 us
    all_to_all x2, blocking collectives: 44.9 us -> 42.2 us  [along_z(): return lax.all_to_all(array, 'ctx', 0, 0, axis_index_groups=z_groups)]
    pallas_call x4 -> x6, Pallas kernels: 9.68 us -> 11.7 us  [call(): pl.pallas_call(kernel, out_shape=[jax.ShapeDtypeStruct(*out) for out in o...]
    pallas_call x1 -> x0, Pallas kernels: 1.44 us -> none  [on_device(): pl.pallas_call(finish_kernel, out_shape=[jax.ShapeDtypeStruct((2 * SEG *...]
    ppermute x4 -> x5, starting transfers between devices: 2.17 us -> 2.27 us  [swap(): return lax.ppermute(array, 'ctx', [(i, i ^ relative) for i in range(32)])]
  transfers between devices with their start and end apart: 8 -> 9, of which waited for: 4 -> 5; matrix products, arithmetic and copies ran while one was open for 0% -> 0% of each run, Pallas kernels for 4% -> 5%
where the time goes in v4:
time: 83.1 us; the launch traced here: 81.6 us
  blocking collectives  42.2 us (51%)
  waiting for transfers between devices  15.2 us (18%)
  Pallas kernels  13.6 us (16%)
  starting transfers between devices  9.77 us (12%)
    all_to_all x2, blocking collectives, along_z(): return lax.all_to_all(array, 'ctx', 0, 0, axis_index_groups=z_groups)  42.2 us
    pallas_call x6, Pallas kernels, call(): pl.pallas_call(kernel, out_shape=[jax.ShapeDtypeStruct(*out) for out in o...  11.7 us
    all_to_all x1, waiting for transfers between devices, along_z(): return lax.all_to_all(array, 'ctx', 0, 0, axis_index_groups=z_groups)  10.3 us
    ppermute x3, starting transfers between devices, swap_wide(): return lax.ppermute(array, ('dp', 'ctx'), pairs)  4.09 us
    all_to_all x1, starting transfers between devices, along_z(): return lax.all_to_all(array, 'ctx', 0, 0, axis_index_groups=z_groups)  3.41 us
    ppermute x3, waiting for transfers between devices, swap_wide(): return lax.ppermute(array, ('dp', 'ctx'), pairs)  3.4 us
    ppermute x5, starting transfers between devices, swap(): return lax.ppermute(array, 'ctx', [(i, i ^ relative) for i in range(32)])  2.27 us
    pallas_call x1, Pallas kernels, on_device(): pl.pallas_call(pack_kernel, out_shape=[jax.ShapeDtypeStruct((PLACES, 2, S...  1.91 us
  transfers between devices with their start and end apart: 9, of which 5 were waited for; matrix products, arithmetic and copies ran while one was open for 0% of the time, Pallas kernels for 5%

profile of v4, /device:TPU:16, one launch (start us, length us, event | category | flops | bytes accessed | tf_op | source)
XLA Modules:
  0.0 81.6 jit_solution(8036116316944261498)
XLA Ops:
  0.6 1.9 %pack.1 = (bf16[8,2,64,256]{3,2,1,0:T(8,128)(2,1)}, bf16[8,2,64,128]{3,2,1,0:T(8,128)(2,1)}, s32[1]{0:T(128)}) custom-call(s32[2]{0:T(128)} %ids_ref.1, bf16[1024,128]{1,0:T(8,128)(2,1)} %bitcast.23, bf16[128,128]{1,0:T(8,128)(2,1)} %bitcast.24, bf16[128,128]{1,0:T(8,128)(2,1)} %bitcast.25), custom_call_target="tpu_custom_call" | custom-call | tf_op jit(solution)/shard_map/pack/pallas_call | solution.py:396
  2.6 26.0 %all_to_all.15.token_ref.own_ref = bf16[8,2,64,256]{3,2,1,0:T(8,128)(2,1)S(1)} all-to-all(bf16[8,2,64,256]{3,2,1,0:T(8,128)(2,1)} %get-tuple-element.20), channel_id=1, replica_groups={{0,16,32,48,64,80,96,112},{4,20,36,52,68,84,100,116},{8,24,40,56,72,88,..., dimensions={0} | all-to-all | bytes 1048576 | tf_op jit(solution)/shard_map/all_to_all | solution.py:392
  28.5 1.5 %collective-permute-start.1 = (bf16[8,2,64,256]{3,2,1,0:T(8,128)(2,1)S(1)}, bf16[8,2,64,256]{3,2,1,0:T(8,128)(2,1)S(1)}, u32[]{:S(2)}, u32[]{:S(2)}) collective-permute-start(bf16[8,2,64,256]{3,2,1,0:T(8,128)(2,1)S(1)} %all_to_all.15.token_ref.own_ref), channel_id=1, source_target_pairs={{0,8},{4,12},{8,0},{12,4},{16,24},{20,28},{24,16},{28,20},{32,40},... | collective-permute-start | bytes 1572872 | tf_op jit(solution)/shard_map/ppermute | solution.py:389
  30.0 3.4 %all-to-all-start.1 = ((bf16[8,2,64,128]{3,2,1,0:T(8,128)(2,1)}), bf16[8,2,64,128]{3,2,1,0:T(8,128)(2,1)S(1)}, u32[]{:S(2)}, u32[]{:S(2)}) async-start(bf16[8,2,64,128]{3,2,1,0:T(8,128)(2,1)} %tie.2), calls=%async_computation.1 | async-start | bytes 524288 | tf_op jit(solution)/shard_map/all_to_all | solution.py:392
  33.4 0.1 collective-permute-start
  33.6 0.0 copy-start
  33.6 0.0 copy-start.1
  33.6 10.3 %all-to-all-done.1.token_ref.rows_ref = bf16[8,2,64,128]{3,2,1,0:T(8,128)(2,1)S(1)} async-done(((bf16[8,2,64,128]{3,2,1,0:T(8,128)(2,1)}), bf16[8,2,64,128]{3,2,1,0:T(8,128)(2,1)S(1)}, u32[]{:S(2)}, u32[]{:S(2)}) %all-to-all-start.1) | async-done | bytes 262176 | tf_op jit(solution)/shard_map/all_to_all | solution.py:392
  43.8 0.0 collective-permute-done.1.value_ref
  43.8 0.0 collective-permute-start.2
  43.8 0.1 pad_add_fusion.at_ref
  43.9 0.0 collective-permute-done.core_ref
  43.9 0.0 copy-done
  43.9 0.0 copy-done.1
  43.9 3.5 %first_half.1 = (f32[4,128,256]{2,1,0:T(8,128)S(1)}, f32[4,1,256]{2,1,0:T(1,128)S(1)}, f32[4,1,256]{2,1,0:T(1,128)S(1)}, f32[4,128,256]{2,1,0:T(8,128)S(1)}, f32...) custom-call(s32[2]{0:T(128)S(1)} %pad_add_fusion.at_ref, ...), custom_call_target="tpu_custom_call" | custom-call | flops 5000000000 | tf_op jit(solution)/shard_map/first_half/pallas_call | solution.py:359
  47.4 0.0 collective-permute-done.2.far_ref
  47.4 6.0 %rest.1 = (bf16[8,2,64,128]{3,2,1,0:T(8,128)(2,1)S(1)}, f32[2,64,128]{2,1,0:T(8,128)S(1)}) custom-call(s32[2]{0:T(128)S(1)} %pad_add_fusion.at_ref, bf16[8,2,64,128]{3,2,1,0:T(8,128)(2,1)S(1)} %all-to-all-done.1.token_ref.rows_ref, bf16[8,2,64,256]{3,2,1,0:T(8,128)(2,1)S(1)} %all_to_all.15.token_ref.own_ref, ...), custom_call_target="tpu_custom_call" | custom-call | flops 10000000000 | tf_op jit(solution)/shard_map/rest/pallas_call | solution.py:359
  53.4 0.6 collective-permute-start.3
  54.0 0.9 %collective-permute-done.3.two_ref = f32[64,128]{1,0:T(8,128)S(1)} collective-permute-done((f32[64,128]{1,0:T(8,128)S(1)}, f32[64,128]{1,0:T(8,128)S(1)}, u32[]{:S(2)}, u32[]{:S(2)}) %collective-permute-start.3) | collective-permute-done | bytes 32800 | tf_op jit(solution)/shard_map/ppermute | solution.py:389
  54.9 2.1 %collective-permute-start.6 = (bf16[64,128]{1,0:T(8,128)(2,1)S(1)}, bf16[64,128]{1,0:T(8,128)(2,1)S(1)}, u32[]{:S(2)}, u32[]{:S(2)}) collective-permute-start(bf16[64,128]{1,0:T(8,128)(2,1)S(1)} %pair.1.a_ref), channel_id=1, source_target_pairs={{0,136},{4,140},{8,128},{12,132},{16,152},{20,156},{24,144},{28,14... | collective-permute-start | bytes 49160 | tf_op jit(solution)/shard_map/ppermute | solution.py:446
  57.0 0.7 collective-permute-start.5
  57.7 1.3 %collective-permute-start.4 = (bf16[64,128]{1,0:T(8,128)(2,1)S(1)}, bf16[64,128]{1,0:T(8,128)(2,1)S(1)}, u32[]{:S(2)}, u32[]{:S(2)}) collective-permute-start(bf16[64,128]{1,0:T(8,128)(2,1)S(1)} %pair.1.a_ref), channel_id=1, source_target_pairs={{0,8},{4,12},{8,0},{12,4},{16,24},{20,28},{24,16},{28,20},{32,40},... | collective-permute-start | bytes 49160 | tf_op jit(solution)/shard_map/ppermute | solution.py:446
  59.0 0.9 %collective-permute-done.6.d_ref = bf16[64,128]{1,0:T(8,128)(2,1)S(1)} collective-permute-done((bf16[64,128]{1,0:T(8,128)(2,1)S(1)}, bf16[64,128]{1,0:T(8,128)(2,1)S(1)}, u32[]{:S(2)}, u32[]{:S(2)}) %collective-permute-start.6) | collective-permute-done | bytes 16416 | tf_op jit(solution)/shard_map/ppermute | solution.py:446
  59.8 2.5 %collective-permute-done.5.c_ref = bf16[64,128]{1,0:T(8,128)(2,1)S(1)} collective-permute-done((bf16[64,128]{1,0:T(8,128)(2,1)S(1)}, bf16[64,128]{1,0:T(8,128)(2,1)S(1)}, u32[]{:S(2)}, u32[]{:S(2)}) %collective-permute-start.5) | collective-permute-done | bytes 16416 | tf_op jit(solution)/shard_map/ppermute | solution.py:446
  62.4 0.0 collective-permute-done.4.b_ref
  62.4 16.3 %all_to_all.16.whole_ref = bf16[8,3,64,128]{3,2,1,0:T(8,128)(2,1)S(1)} all-to-all(bf16[8,3,64,128]{3,2,1,0:T(8,128)(2,1)S(1)} %share.1), channel_id=1, replica_groups={{0,16,32,48,64,80,96,112},{4,20,36,52,68,84,100,116},{8,24,40,56,72,88,..., dimensions={0} | all-to-all | bytes 786432 | tf_op jit(solution)/shard_map/all_to_all | solution.py:392
  78.7 0.1 collective-permute-start.7
  78.8 0.7 student_rows.1.rows_ref
  79.5 0.6 collective-permute-done.7.other_ref
  80.2 1.5 %finish.1 = (bf16[1024,128]{1,0:T(8,128)(2,1)}, f32[8,64,128]{2,1,0:T(8,128)}, f32[8,64,128]{2,1,0:T(8,128)}) custom-call(s32[2]{0:T(128)S(1)} %pad_add_fusion.at_ref, bf16[1024,128]{1,0:T(8,128)(2,1)S(1)} %student_rows.1.rows_ref, bf16[8,3,64,128]{3,2,1,0:T(8,128)(2,1)S(1)} %all_to_all.16.whole_ref, bf16[8,64,128]{2,1,0:T(8,128)(2,1)S(1)} %collective-permute-done.7.other_ref), custom_call_target="tpu_custom_call" | custom-call | tf_op jit(solution)/shard_map/finish/pallas_call | solution.py:359
  (6 shorter events, 0.1 us)
Async XLA Ops:
  28.5 15.3 %collective-permute-start.1 = (bf16[8,2,64,256]{3,2,1,0:T(8,128)(2,1)S(1)}, bf16[8,2,64,256]{3,2,1,0:T(8,128)(2,1)S(1)}, u32[]{:S(2)}, u32[]{:S(2)}) collective-permute-start(bf16[8,2,64,256]{3,2,1,0:T(8,128)(2,1)S(1)} %all_to_all.15.token_ref.own_ref), channel_id=1, source_target_pairs={{0,8},{4,12},{8,0},{12,4},{16,24},{20,28},{24,16},{28,20},{32,40},... | collective-permute-start | bytes 1572872 | tf_op jit(solution)/shard_map/ppermute | solution.py:389
  30.0 13.8 %all-to-all-start.1 = ((bf16[8,2,64,128]{3,2,1,0:T(8,128)(2,1)}), bf16[8,2,64,128]{3,2,1,0:T(8,128)(2,1)S(1)}, u32[]{:S(2)}, u32[]{:S(2)}) async-start(bf16[8,2,64,128]{3,2,1,0:T(8,128)(2,1)} %tie.2), calls=%async_computation.1 | async-start | bytes 524288 | tf_op jit(solution)/shard_map/all_to_all | solution.py:392
  33.4 10.5 %collective-permute-start = (bf16[8,2,64,256]{3,2,1,0:T(8,128)(2,1)S(1)}, bf16[8,2,64,256]{3,2,1,0:T(8,128)(2,1)S(1)}, u32[]{:S(2)}, u32[]{:S(2)}) collective-permute-start(bf16[8,2,64,256]{3,2,1,0:T(8,128)(2,1)S(1)} %all_to_all.15.token_ref.own_ref), channel_id=1, source_target_pairs={{0,4},{4,0},{8,12},{12,8},{16,20},{20,16},{24,28},{28,24},{32,36},... | collective-permute-start | bytes 1572872 | tf_op jit(solution)/shard_map/ppermute | solution.py:389
  33.6 10.4 %copy-start = (bf16[8,128,64]{1,2,0:T(8,128)(2,1)S(1)}, bf16[8,128,64]{1,2,0:T(8,128)(2,1)}, u32[]{:S(2)}) copy-start(bf16[8,128,64]{1,2,0:T(8,128)(2,1)} %param.10) | copy-start | bytes 393220
  33.6 10.4 %copy-start.1 = (bf16[8,128,64]{1,2,0:T(8,128)(2,1)S(1)}, bf16[8,128,64]{1,2,0:T(8,128)(2,1)}, u32[]{:S(2)}) copy-start(bf16[8,128,64]{1,2,0:T(8,128)(2,1)} %param.11) | copy-start | bytes 393220
  43.8 3.6 %collective-permute-start.2 = (bf16[8,2,64,256]{3,2,1,0:T(8,128)(2,1)S(1)}, bf16[8,2,64,256]{3,2,1,0:T(8,128)(2,1)S(1)}, u32[]{:S(2)}, u32[]{:S(2)}) collective-permute-start(bf16[8,2,64,256]{3,2,1,0:T(8,128)(2,1)S(1)} %tie.3.x_ref), channel_id=1, source_target_pairs={{0,4},{4,0},{8,12},{12,8},{16,20},{20,16},{24,28},{28,24},{32,36},... | collective-permute-start | bytes 1572872 | tf_op jit(solution)/shard_map/ppermute | solution.py:389
  53.4 1.4 %collective-permute-start.3 = (f32[64,128]{1,0:T(8,128)S(1)}, f32[64,128]{1,0:T(8,128)S(1)}, u32[]{:S(2)}, u32[]{:S(2)}) collective-permute-start(f32[64,128]{1,0:T(8,128)S(1)} %get-tuple-element.39), channel_id=1, source_target_pairs={{0,4},{4,0},{8,12},{12,8},{16,20},{20,16},{24,28},{28,24},{32,36},... | collective-permute-start | bytes 98312 | tf_op jit(solution)/shard_map/ppermute | solution.py:389
  54.9 4.9 %collective-permute-start.6 = (bf16[64,128]{1,0:T(8,128)(2,1)S(1)}, bf16[64,128]{1,0:T(8,128)(2,1)S(1)}, u32[]{:S(2)}, u32[]{:S(2)}) collective-permute-start(bf16[64,128]{1,0:T(8,128)(2,1)S(1)} %pair.1.a_ref), channel_id=1, source_target_pairs={{0,136},{4,140},{8,128},{12,132},{16,152},{20,156},{24,144},{28,14... | collective-permute-start | bytes 49160 | tf_op jit(solution)/shard_map/ppermute | solution.py:446
  57.0 5.4 %collective-permute-start.5 = (bf16[64,128]{1,0:T(8,128)(2,1)S(1)}, bf16[64,128]{1,0:T(8,128)(2,1)S(1)}, u32[]{:S(2)}, u32[]{:S(2)}) collective-permute-start(bf16[64,128]{1,0:T(8,128)(2,1)S(1)} %pair.1.a_ref), channel_id=1, source_target_pairs={{0,128},{4,132},{8,136},{12,140},{16,144},{20,148},{24,152},{28,15... | collective-permute-start | bytes 49160 | tf_op jit(solution)/shard_map/ppermute | solution.py:446
  57.7 4.7 %collective-permute-start.4 = (bf16[64,128]{1,0:T(8,128)(2,1)S(1)}, bf16[64,128]{1,0:T(8,128)(2,1)S(1)}, u32[]{:S(2)}, u32[]{:S(2)}) collective-permute-start(bf16[64,128]{1,0:T(8,128)(2,1)S(1)} %pair.1.a_ref), channel_id=1, source_target_pairs={{0,8},{4,12},{8,0},{12,4},{16,24},{20,28},{24,16},{28,20},{32,40},... | collective-permute-start | bytes 49160 | tf_op jit(solution)/shard_map/ppermute | solution.py:446
  78.7 1.4 %collective-permute-start.7 = (bf16[8,64,128]{2,1,0:T(8,128)(2,1)S(1)}, bf16[8,64,128]{2,1,0:T(8,128)(2,1)S(1)}, u32[]{:S(2)}, u32[]{:S(2)}) collective-permute-start(bf16[8,64,128]{2,1,0:T(8,128)(2,1)S(1)} %slice_bitcast_fusion), channel_id=1, source_target_pairs={{0,4},{4,0},{8,12},{12,8},{16,20},{20,16},{24,28},{28,24},{32,36},... | collective-permute-start | bytes 393224 | tf_op jit(solution)/shard_map/ppermute | solution.py:389

commit v5 on v4

--- a/solution.py
+++ b/solution.py
@@ -9,6 +9,8 @@
 
 PLACES = 8
 MEMBERS = 4
+ORDER = (0, 2, 4, 6, 1, 3, 5, 7)
+SLOT = tuple(ORDER.index(place) for place in range(PLACES))
 SEG = 64
 HD = 128
 FD = 64
@@ -66,7 +68,7 @@
 
 
 def where_is(chunk):
-    return (chunk, 0) if chunk < PLACES else (2 * PLACES - 1 - chunk, 1)
+    return (SLOT[chunk], 0) if chunk < PLACES else (SLOT[2 * PLACES - 1 - chunk], 1)
 
 
 def block_rows(refs, block, columns):
@@ -110,7 +112,7 @@
     for late in range(2):
         for place in range(PLACES):
             rows = pl.ds(half_rows(late) * PLACES + place, SEG, stride=PLACES)
-            outq_ref[place, late] = wide[rows].astype(BF16)
+            outq_ref[SLOT[place], late] = wide[rows].astype(BF16)
 
 
 def tie_kernel(value_ref, token_ref, out_ref):
@@ -136,7 +138,7 @@
         start = pl.multiple_of(jnp.where(swapped, SEG - SEG * late, SEG * late), SEG)
         for place in range(PLACES):
             rows = pl.ds(start * PLACES + place, SEG, stride=PLACES)
-            wide[rows] = whole_ref[place, late].astype(F32)
+            wide[rows] = whole_ref[SLOT[place], late].astype(F32)
     student_ref[...] = wide[...].astype(BF16)
 
 
@@ -144,8 +146,8 @@
     odd = at_ref[1] % 2 == 1
     student_ref[...] = rows_ref[...]
     for place in range(PLACES):
-        mine = whole_ref[place, 2].astype(F32)
-        other = other_ref[place].astype(F32)
+        mine = whole_ref[SLOT[place], 2].astype(F32)
+        other = other_ref[SLOT[place]].astype(F32)
         gq_ref[place] = jnp.where(odd, other, mine)
         gk_ref[place] = jnp.where(odd, mine, other)
 
@@ -383,7 +385,7 @@
 def on_device(queries, keys, values, segment_ids, feat_query, feat_key):
     spot = lax.axis_index("ctx")
     place, member = spot // MEMBERS, spot % MEMBERS
-    z_groups = [[j + MEMBERS * k for k in range(PLACES)] for j in range(MEMBERS)]
+    z_groups = [[j + MEMBERS * k for k in ORDER] for j in range(MEMBERS)]
 
     def swap(array, relative):
         return lax.ppermute(array, "ctx", [(i, i ^ relative) for i in range(32)])

time: 83.1 us -> 80.4 us (0.968)
  blocking collectives: 42.2 us -> 40.4 us
  waiting for transfers between devices: 15.2 us -> 13.6 us
    all_to_all x2, blocking collectives: 42.2 us -> 40.4 us  [along_z(): return lax.all_to_all(array, 'ctx', 0, 0, axis_index_groups=z_groups)]
    all_to_all x1, waiting for transfers between devices: 10.3 us -> 8.66 us  [along_z(): return lax.all_to_all(array, 'ctx', 0, 0, axis_index_groups=z_groups)]
where the time goes in v5:
time: 80.4 us; the launch traced here: 78.9 us
  blocking collectives  40.4 us (50%)
  Pallas kernels  13.6 us (17%)
  waiting for transfers between devices  13.6 us (17%)
  starting transfers between devices  10.5 us (13%)
    all_to_all x2, blocking collectives, along_z(): return lax.all_to_all(array, 'ctx', 0, 0, axis_index_groups=z_groups)  40.4 us
    pallas_call x6, Pallas kernels, call(): pl.pallas_call(kernel, out_shape=[jax.ShapeDtypeStruct(*out) for out in o...  11.6 us
    all_to_all x1, waiting for transfers between devices, along_z(): return lax.all_to_all(array, 'ctx', 0, 0, axis_index_groups=z_groups)  8.66 us
    all_to_all x1, starting transfers between devices, along_z(): return lax.all_to_all(array, 'ctx', 0, 0, axis_index_groups=z_groups)  4.21 us
    ppermute x3, starting transfers between devices, swap_wide(): return lax.ppermute(array, ('dp', 'ctx'), pairs)  4.09 us
    ppermute x3, waiting for transfers between devices, swap_wide(): return lax.ppermute(array, ('dp', 'ctx'), pairs)  3.41 us
    ppermute x5, starting transfers between devices, swap(): return lax.ppermute(array, 'ctx', [(i, i ^ relative) for i in range(32)])  2.18 us
    pallas_call x1, Pallas kernels, on_device(): pl.pallas_call(pack_kernel, out_shape=[jax.ShapeDtypeStruct((PLACES, 2, S...  1.91 us
  transfers between devices with their start and end apart: 9, of which 5 were waited for; matrix products, arithmetic and copies ran while one was open for 0% of the time, Pallas kernels for 5%

profile of v5, /device:TPU:16, one launch (start us, length us, event | category | flops | bytes accessed | tf_op | source)
XLA Modules:
  0.0 78.9 jit_solution(17983562046969014389)
XLA Ops:
  0.6 1.9 %pack.1 = (bf16[8,2,64,256]{3,2,1,0:T(8,128)(2,1)}, bf16[8,2,64,128]{3,2,1,0:T(8,128)(2,1)}, s32[1]{0:T(128)}) custom-call(s32[2]{0:T(128)} %ids_ref.1, bf16[1024,128]{1,0:T(8,128)(2,1)} %bitcast.23, bf16[128,128]{1,0:T(8,128)(2,1)} %bitcast.24, bf16[128,128]{1,0:T(8,128)(2,1)} %bitcast.25), custom_call_target="tpu_custom_call" | custom-call | tf_op jit(solution)/shard_map/pack/pallas_call | solution.py:398
  2.6 23.6 %all_to_all.15.token_ref.own_ref = bf16[8,2,64,256]{3,2,1,0:T(8,128)(2,1)S(1)} all-to-all(bf16[8,2,64,256]{3,2,1,0:T(8,128)(2,1)} %get-tuple-element.20), channel_id=1, replica_groups={{0,32,64,96,16,48,80,112},{4,36,68,100,20,52,84,116},{8,40,72,104,24,56..., dimensions={0} | all-to-all | bytes 1048576 | tf_op jit(solution)/shard_map/all_to_all | solution.py:394
  26.2 1.5 %collective-permute-start.1 = (bf16[8,2,64,256]{3,2,1,0:T(8,128)(2,1)S(1)}, bf16[8,2,64,256]{3,2,1,0:T(8,128)(2,1)S(1)}, u32[]{:S(2)}, u32[]{:S(2)}) collective-permute-start(bf16[8,2,64,256]{3,2,1,0:T(8,128)(2,1)S(1)} %all_to_all.15.token_ref.own_ref), channel_id=1, source_target_pairs={{0,8},{4,12},{8,0},{12,4},{16,24},{20,28},{24,16},{28,20},{32,40},... | collective-permute-start | bytes 1572872 | tf_op jit(solution)/shard_map/ppermute | solution.py:391
  27.7 4.2 %all-to-all-start.1 = ((bf16[8,2,64,128]{3,2,1,0:T(8,128)(2,1)}), bf16[8,2,64,128]{3,2,1,0:T(8,128)(2,1)S(1)}, u32[]{:S(2)}, u32[]{:S(2)}) async-start(bf16[8,2,64,128]{3,2,1,0:T(8,128)(2,1)} %tie.2), calls=%async_computation.1 | async-start | bytes 524288 | tf_op jit(solution)/shard_map/all_to_all | solution.py:394
  31.9 0.0 collective-permute-start
  31.9 0.0 copy-start
  31.9 0.0 copy-start.1
  31.9 8.7 %all-to-all-done.1.token_ref.rows_ref = bf16[8,2,64,128]{3,2,1,0:T(8,128)(2,1)S(1)} async-done(((bf16[8,2,64,128]{3,2,1,0:T(8,128)(2,1)}), bf16[8,2,64,128]{3,2,1,0:T(8,128)(2,1)S(1)}, u32[]{:S(2)}, u32[]{:S(2)}) %all-to-all-start.1) | async-done | bytes 262176 | tf_op jit(solution)/shard_map/all_to_all | solution.py:394
  40.6 0.0 collective-permute-done.1.value_ref
  40.6 0.0 collective-permute-start.2
  40.6 0.1 pad_add_fusion.at_ref
  40.7 0.0 collective-permute-done.core_ref
  40.7 0.0 copy-done
  40.7 0.0 copy-done.1
  40.7 3.5 %first_half.1 = (f32[4,128,256]{2,1,0:T(8,128)S(1)}, f32[4,1,256]{2,1,0:T(1,128)S(1)}, f32[4,1,256]{2,1,0:T(1,128)S(1)}, f32[4,128,256]{2,1,0:T(8,128)S(1)}, f32...) custom-call(s32[2]{0:T(128)S(1)} %pad_add_fusion.at_ref, ...), custom_call_target="tpu_custom_call" | custom-call | flops 5000000000 | tf_op jit(solution)/shard_map/first_half/pallas_call | solution.py:361
  44.1 0.0 collective-permute-done.2.far_ref
  44.2 6.0 %rest.1 = (bf16[8,2,64,128]{3,2,1,0:T(8,128)(2,1)S(1)}, f32[2,64,128]{2,1,0:T(8,128)S(1)}) custom-call(s32[2]{0:T(128)S(1)} %pad_add_fusion.at_ref, bf16[8,2,64,128]{3,2,1,0:T(8,128)(2,1)S(1)} %all-to-all-done.1.token_ref.rows_ref, bf16[8,2,64,256]{3,2,1,0:T(8,128)(2,1)S(1)} %all_to_all.15.token_ref.own_ref, ...), custom_call_target="tpu_custom_call" | custom-call | flops 10000000000 | tf_op jit(solution)/shard_map/rest/pallas_call | solution.py:361
  50.2 0.6 collective-permute-start.3
  50.8 0.9 %collective-permute-done.3.two_ref = f32[64,128]{1,0:T(8,128)S(1)} collective-permute-done((f32[64,128]{1,0:T(8,128)S(1)}, f32[64,128]{1,0:T(8,128)S(1)}, u32[]{:S(2)}, u32[]{:S(2)}) %collective-permute-start.3) | collective-permute-done | bytes 32800 | tf_op jit(solution)/shard_map/ppermute | solution.py:391
  51.7 2.1 %collective-permute-start.6 = (bf16[64,128]{1,0:T(8,128)(2,1)S(1)}, bf16[64,128]{1,0:T(8,128)(2,1)S(1)}, u32[]{:S(2)}, u32[]{:S(2)}) collective-permute-start(bf16[64,128]{1,0:T(8,128)(2,1)S(1)} %pair.1.a_ref), channel_id=1, source_target_pairs={{0,136},{4,140},{8,128},{12,132},{16,152},{20,156},{24,144},{28,14... | collective-permute-start | bytes 49160 | tf_op jit(solution)/shard_map/ppermute | solution.py:448
  53.7 0.7 collective-permute-start.5
  54.5 1.3 %collective-permute-start.4 = (bf16[64,128]{1,0:T(8,128)(2,1)S(1)}, bf16[64,128]{1,0:T(8,128)(2,1)S(1)}, u32[]{:S(2)}, u32[]{:S(2)}) collective-permute-start(bf16[64,128]{1,0:T(8,128)(2,1)S(1)} %pair.1.a_ref), channel_id=1, source_target_pairs={{0,8},{4,12},{8,0},{12,4},{16,24},{20,28},{24,16},{28,20},{32,40},... | collective-permute-start | bytes 49160 | tf_op jit(solution)/shard_map/ppermute | solution.py:448
  55.7 0.9 %collective-permute-done.6.d_ref = bf16[64,128]{1,0:T(8,128)(2,1)S(1)} collective-permute-done((bf16[64,128]{1,0:T(8,128)(2,1)S(1)}, bf16[64,128]{1,0:T(8,128)(2,1)S(1)}, u32[]{:S(2)}, u32[]{:S(2)}) %collective-permute-start.6) | collective-permute-done | bytes 16416 | tf_op jit(solution)/shard_map/ppermute | solution.py:448
  56.6 2.5 %collective-permute-done.5.c_ref = bf16[64,128]{1,0:T(8,128)(2,1)S(1)} collective-permute-done((bf16[64,128]{1,0:T(8,128)(2,1)S(1)}, bf16[64,128]{1,0:T(8,128)(2,1)S(1)}, u32[]{:S(2)}, u32[]{:S(2)}) %collective-permute-start.5) | collective-permute-done | bytes 16416 | tf_op jit(solution)/shard_map/ppermute | solution.py:448
  59.1 0.0 collective-permute-done.4.b_ref
  59.2 16.8 %all_to_all.16.whole_ref = bf16[8,3,64,128]{3,2,1,0:T(8,128)(2,1)S(1)} all-to-all(bf16[8,3,64,128]{3,2,1,0:T(8,128)(2,1)S(1)} %share.1), channel_id=1, replica_groups={{0,32,64,96,16,48,80,112},{4,36,68,100,20,52,84,116},{8,40,72,104,24,56..., dimensions={0} | all-to-all | bytes 786432 | tf_op jit(solution)/shard_map/all_to_all | solution.py:394
  76.0 0.1 collective-permute-start.7
  76.1 0.7 student_rows.1.rows_ref
  76.8 0.6 collective-permute-done.7.other_ref
  77.4 1.5 %finish.1 = (bf16[1024,128]{1,0:T(8,128)(2,1)}, f32[8,64,128]{2,1,0:T(8,128)}, f32[8,64,128]{2,1,0:T(8,128)}) custom-call(s32[2]{0:T(128)S(1)} %pad_add_fusion.at_ref, bf16[1024,128]{1,0:T(8,128)(2,1)S(1)} %student_rows.1.rows_ref, bf16[8,3,64,128]{3,2,1,0:T(8,128)(2,1)S(1)} %all_to_all.16.whole_ref, bf16[8,64,128]{2,1,0:T(8,128)(2,1)S(1)} %collective-permute-done.7.other_ref), custom_call_target="tpu_custom_call" | custom-call | tf_op jit(solution)/shard_map/finish/pallas_call | solution.py:361
  (6 shorter events, 0.1 us)
Async XLA Ops:
  26.2 14.4 %collective-permute-start.1 = (bf16[8,2,64,256]{3,2,1,0:T(8,128)(2,1)S(1)}, bf16[8,2,64,256]{3,2,1,0:T(8,128)(2,1)S(1)}, u32[]{:S(2)}, u32[]{:S(2)}) collective-permute-start(bf16[8,2,64,256]{3,2,1,0:T(8,128)(2,1)S(1)} %all_to_all.15.token_ref.own_ref), channel_id=1, source_target_pairs={{0,8},{4,12},{8,0},{12,4},{16,24},{20,28},{24,16},{28,20},{32,40},... | collective-permute-start | bytes 1572872 | tf_op jit(solution)/shard_map/ppermute | solution.py:391
  27.7 12.9 %all-to-all-start.1 = ((bf16[8,2,64,128]{3,2,1,0:T(8,128)(2,1)}), bf16[8,2,64,128]{3,2,1,0:T(8,128)(2,1)S(1)}, u32[]{:S(2)}, u32[]{:S(2)}) async-start(bf16[8,2,64,128]{3,2,1,0:T(8,128)(2,1)} %tie.2), calls=%async_computation.1 | async-start | bytes 524288 | tf_op jit(solution)/shard_map/all_to_all | solution.py:394
  31.9 8.8 %collective-permute-start = (bf16[8,2,64,256]{3,2,1,0:T(8,128)(2,1)S(1)}, bf16[8,2,64,256]{3,2,1,0:T(8,128)(2,1)S(1)}, u32[]{:S(2)}, u32[]{:S(2)}) collective-permute-start(bf16[8,2,64,256]{3,2,1,0:T(8,128)(2,1)S(1)} %all_to_all.15.token_ref.own_ref), channel_id=1, source_target_pairs={{0,4},{4,0},{8,12},{12,8},{16,20},{20,16},{24,28},{28,24},{32,36},... | collective-permute-start | bytes 1572872 | tf_op jit(solution)/shard_map/ppermute | solution.py:391
  31.9 8.8 %copy-start = (bf16[8,128,64]{1,2,0:T(8,128)(2,1)S(1)}, bf16[8,128,64]{1,2,0:T(8,128)(2,1)}, u32[]{:S(2)}) copy-start(bf16[8,128,64]{1,2,0:T(8,128)(2,1)} %param.10) | copy-start | bytes 393220
  31.9 8.8 %copy-start.1 = (bf16[8,128,64]{1,2,0:T(8,128)(2,1)S(1)}, bf16[8,128,64]{1,2,0:T(8,128)(2,1)}, u32[]{:S(2)}) copy-start(bf16[8,128,64]{1,2,0:T(8,128)(2,1)} %param.11) | copy-start | bytes 393220
  40.6 3.6 %collective-permute-start.2 = (bf16[8,2,64,256]{3,2,1,0:T(8,128)(2,1)S(1)}, bf16[8,2,64,256]{3,2,1,0:T(8,128)(2,1)S(1)}, u32[]{:S(2)}, u32[]{:S(2)}) collective-permute-start(bf16[8,2,64,256]{3,2,1,0:T(8,128)(2,1)S(1)} %tie.3.x_ref), channel_id=1, source_target_pairs={{0,4},{4,0},{8,12},{12,8},{16,20},{20,16},{24,28},{28,24},{32,36},... | collective-permute-start | bytes 1572872 | tf_op jit(solution)/shard_map/ppermute | solution.py:391
  50.2 1.5 %collective-permute-start.3 = (f32[64,128]{1,0:T(8,128)S(1)}, f32[64,128]{1,0:T(8,128)S(1)}, u32[]{:S(2)}, u32[]{:S(2)}) collective-permute-start(f32[64,128]{1,0:T(8,128)S(1)} %get-tuple-element.39), channel_id=1, source_target_pairs={{0,4},{4,0},{8,12},{12,8},{16,20},{20,16},{24,28},{28,24},{32,36},... | collective-permute-start | bytes 98312 | tf_op jit(solution)/shard_map/ppermute | solution.py:391
  51.7 4.9 %collective-permute-start.6 = (bf16[64,128]{1,0:T(8,128)(2,1)S(1)}, bf16[64,128]{1,0:T(8,128)(2,1)S(1)}, u32[]{:S(2)}, u32[]{:S(2)}) collective-permute-start(bf16[64,128]{1,0:T(8,128)(2,1)S(1)} %pair.1.a_ref), channel_id=1, source_target_pairs={{0,136},{4,140},{8,128},{12,132},{16,152},{20,156},{24,144},{28,14... | collective-permute-start | bytes 49160 | tf_op jit(solution)/shard_map/ppermute | solution.py:448
  53.7 5.4 %collective-permute-start.5 = (bf16[64,128]{1,0:T(8,128)(2,1)S(1)}, bf16[64,128]{1,0:T(8,128)(2,1)S(1)}, u32[]{:S(2)}, u32[]{:S(2)}) collective-permute-start(bf16[64,128]{1,0:T(8,128)(2,1)S(1)} %pair.1.a_ref), channel_id=1, source_target_pairs={{0,128},{4,132},{8,136},{12,140},{16,144},{20,148},{24,152},{28,15... | collective-permute-start | bytes 49160 | tf_op jit(solution)/shard_map/ppermute | solution.py:448
  54.5 4.7 %collective-permute-start.4 = (bf16[64,128]{1,0:T(8,128)(2,1)S(1)}, bf16[64,128]{1,0:T(8,128)(2,1)S(1)}, u32[]{:S(2)}, u32[]{:S(2)}) collective-permute-start(bf16[64,128]{1,0:T(8,128)(2,1)S(1)} %pair.1.a_ref), channel_id=1, source_target_pairs={{0,8},{4,12},{8,0},{12,4},{16,24},{20,28},{24,16},{28,20},{32,40},... | collective-permute-start | bytes 49160 | tf_op jit(solution)/shard_map/ppermute | solution.py:448
  76.0 1.4 %collective-permute-start.7 = (bf16[8,64,128]{2,1,0:T(8,128)(2,1)S(1)}, bf16[8,64,128]{2,1,0:T(8,128)(2,1)S(1)}, u32[]{:S(2)}, u32[]{:S(2)}) collective-permute-start(bf16[8,64,128]{2,1,0:T(8,128)(2,1)S(1)} %slice_bitcast_fusion), channel_id=1, source_target_pairs={{0,4},{4,0},{8,12},{12,8},{16,20},{20,16},{24,28},{28,24},{32,36},... | collective-permute-start | bytes 393224 | tf_op jit(solution)/shard_map/ppermute | solution.py:391

commit v6 on v5

--- a/solution.py
+++ b/solution.py
@@ -9,7 +9,7 @@
 
 PLACES = 8
 MEMBERS = 4
-ORDER = (0, 2, 4, 6, 1, 3, 5, 7)
+ORDER = (0, 2, 4, 6, 7, 1, 3, 5)
 SLOT = tuple(ORDER.index(place) for place in range(PLACES))
 SEG = 64
 HD = 128

time: 80.4 us -> 79.8 us (level)
  no operation moved by 1% of the time
where the time goes in v6:
time: 79.8 us; the launch traced here: 78.3 us
  blocking collectives  40 us (50%)
  waiting for transfers between devices  14 us (18%)
  Pallas kernels  13.6 us (17%)
  starting transfers between devices  9.87 us (12%)
    all_to_all x2, blocking collectives, along_z(): return lax.all_to_all(array, 'ctx', 0, 0, axis_index_groups=z_groups)  40 us
    pallas_call x6, Pallas kernels, call(): pl.pallas_call(kernel, out_shape=[jax.ShapeDtypeStruct(*out) for out in o...  11.6 us
    all_to_all x1, waiting for transfers between devices, along_z(): return lax.all_to_all(array, 'ctx', 0, 0, axis_index_groups=z_groups)  9.08 us
    ppermute x3, starting transfers between devices, swap_wide(): return lax.ppermute(array, ('dp', 'ctx'), pairs)  4.09 us
    all_to_all x1, starting transfers between devices, along_z(): return lax.all_to_all(array, 'ctx', 0, 0, axis_index_groups=z_groups)  3.59 us
    ppermute x3, waiting for transfers between devices, swap_wide(): return lax.ppermute(array, ('dp', 'ctx'), pairs)  3.4 us
    ppermute x5, starting transfers between devices, swap(): return lax.ppermute(array, 'ctx', [(i, i ^ relative) for i in range(32)])  2.19 us
    pallas_call x1, Pallas kernels, on_device(): pl.pallas_call(pack_kernel, out_shape=[jax.ShapeDtypeStruct((PLACES, 2, S...  1.91 us
  transfers between devices with their start and end apart: 9, of which 5 were waited for; matrix products, arithmetic and copies ran while one was open for 0% of the time, Pallas kernels for 5%

profile of v6, /device:TPU:16, one launch (start us, length us, event | category | flops | bytes accessed | tf_op | source)
XLA Modules:
  0.0 78.3 jit_solution(4406941264109425227)
XLA Ops:
  0.6 1.9 %pack.1 = (bf16[8,2,64,256]{3,2,1,0:T(8,128)(2,1)}, bf16[8,2,64,128]{3,2,1,0:T(8,128)(2,1)}, s32[1]{0:T(128)}) custom-call(s32[2]{0:T(128)} %ids_ref.1, bf16[1024,128]{1,0:T(8,128)(2,1)} %bitcast.23, bf16[128,128]{1,0:T(8,128)(2,1)} %bitcast.24, bf16[128,128]{1,0:T(8,128)(2,1)} %bitcast.25), custom_call_target="tpu_custom_call" | custom-call | tf_op jit(solution)/shard_map/pack/pallas_call | solution.py:398
  2.6 24.2 %all_to_all.15.token_ref.own_ref = bf16[8,2,64,256]{3,2,1,0:T(8,128)(2,1)S(1)} all-to-all(bf16[8,2,64,256]{3,2,1,0:T(8,128)(2,1)} %get-tuple-element.20), channel_id=1, replica_groups={{0,32,64,96,112,16,48,80},{4,36,68,100,116,20,52,84},{8,40,72,104,120,2..., dimensions={0} | all-to-all | bytes 1048576 | tf_op jit(solution)/shard_map/all_to_all | solution.py:394
  26.8 1.5 %collective-permute-start.1 = (bf16[8,2,64,256]{3,2,1,0:T(8,128)(2,1)S(1)}, bf16[8,2,64,256]{3,2,1,0:T(8,128)(2,1)S(1)}, u32[]{:S(2)}, u32[]{:S(2)}) collective-permute-start(bf16[8,2,64,256]{3,2,1,0:T(8,128)(2,1)S(1)} %all_to_all.15.token_ref.own_ref), channel_id=1, source_target_pairs={{0,8},{4,12},{8,0},{12,4},{16,24},{20,28},{24,16},{28,20},{32,40},... | collective-permute-start | bytes 1572872 | tf_op jit(solution)/shard_map/ppermute | solution.py:391
  28.3 3.6 %all-to-all-start.1 = ((bf16[8,2,64,128]{3,2,1,0:T(8,128)(2,1)}), bf16[8,2,64,128]{3,2,1,0:T(8,128)(2,1)S(1)}, u32[]{:S(2)}, u32[]{:S(2)}) async-start(bf16[8,2,64,128]{3,2,1,0:T(8,128)(2,1)} %tie.2), calls=%async_computation.1 | async-start | bytes 524288 | tf_op jit(solution)/shard_map/all_to_all | solution.py:394
  31.9 0.0 collective-permute-start
  31.9 0.0 copy-start
  31.9 0.0 copy-start.1
  31.9 9.1 %all-to-all-done.1.token_ref.rows_ref = bf16[8,2,64,128]{3,2,1,0:T(8,128)(2,1)S(1)} async-done(((bf16[8,2,64,128]{3,2,1,0:T(8,128)(2,1)}), bf16[8,2,64,128]{3,2,1,0:T(8,128)(2,1)S(1)}, u32[]{:S(2)}, u32[]{:S(2)}) %all-to-all-start.1) | async-done | bytes 262176 | tf_op jit(solution)/shard_map/all_to_all | solution.py:394
  41.0 0.0 collective-permute-done.1.value_ref
  41.0 0.0 collective-permute-start.2
  41.0 0.1 pad_add_fusion.at_ref
  41.1 0.0 collective-permute-done.core_ref
  41.1 0.0 copy-done
  41.1 0.0 copy-done.1
  41.1 3.5 %first_half.1 = (f32[4,128,256]{2,1,0:T(8,128)S(1)}, f32[4,1,256]{2,1,0:T(1,128)S(1)}, f32[4,1,256]{2,1,0:T(1,128)S(1)}, f32[4,128,256]{2,1,0:T(8,128)S(1)}, f32...) custom-call(s32[2]{0:T(128)S(1)} %pad_add_fusion.at_ref, ...), custom_call_target="tpu_custom_call" | custom-call | flops 5000000000 | tf_op jit(solution)/shard_map/first_half/pallas_call | solution.py:361
  44.6 0.0 collective-permute-done.2.far_ref
  44.6 6.0 %rest.1 = (bf16[8,2,64,128]{3,2,1,0:T(8,128)(2,1)S(1)}, f32[2,64,128]{2,1,0:T(8,128)S(1)}) custom-call(s32[2]{0:T(128)S(1)} %pad_add_fusion.at_ref, bf16[8,2,64,128]{3,2,1,0:T(8,128)(2,1)S(1)} %all-to-all-done.1.token_ref.rows_ref, bf16[8,2,64,256]{3,2,1,0:T(8,128)(2,1)S(1)} %all_to_all.15.token_ref.own_ref, ...), custom_call_target="tpu_custom_call" | custom-call | flops 10000000000 | tf_op jit(solution)/shard_map/rest/pallas_call | solution.py:361
  50.6 0.6 collective-permute-start.3
  51.2 0.9 %collective-permute-done.3.two_ref = f32[64,128]{1,0:T(8,128)S(1)} collective-permute-done((f32[64,128]{1,0:T(8,128)S(1)}, f32[64,128]{1,0:T(8,128)S(1)}, u32[]{:S(2)}, u32[]{:S(2)}) %collective-permute-start.3) | collective-permute-done | bytes 32800 | tf_op jit(solution)/shard_map/ppermute | solution.py:391
  52.1 2.1 %collective-permute-start.6 = (bf16[64,128]{1,0:T(8,128)(2,1)S(1)}, bf16[64,128]{1,0:T(8,128)(2,1)S(1)}, u32[]{:S(2)}, u32[]{:S(2)}) collective-permute-start(bf16[64,128]{1,0:T(8,128)(2,1)S(1)} %pair.1.a_ref), channel_id=1, source_target_pairs={{0,136},{4,140},{8,128},{12,132},{16,152},{20,156},{24,144},{28,14... | collective-permute-start | bytes 49160 | tf_op jit(solution)/shard_map/ppermute | solution.py:448
  54.2 0.7 collective-permute-start.5
  54.9 1.3 %collective-permute-start.4 = (bf16[64,128]{1,0:T(8,128)(2,1)S(1)}, bf16[64,128]{1,0:T(8,128)(2,1)S(1)}, u32[]{:S(2)}, u32[]{:S(2)}) collective-permute-start(bf16[64,128]{1,0:T(8,128)(2,1)S(1)} %pair.1.a_ref), channel_id=1, source_target_pairs={{0,8},{4,12},{8,0},{12,4},{16,24},{20,28},{24,16},{28,20},{32,40},... | collective-permute-start | bytes 49160 | tf_op jit(solution)/shard_map/ppermute | solution.py:448
  56.2 0.9 %collective-permute-done.6.d_ref = bf16[64,128]{1,0:T(8,128)(2,1)S(1)} collective-permute-done((bf16[64,128]{1,0:T(8,128)(2,1)S(1)}, bf16[64,128]{1,0:T(8,128)(2,1)S(1)}, u32[]{:S(2)}, u32[]{:S(2)}) %collective-permute-start.6) | collective-permute-done | bytes 16416 | tf_op jit(solution)/shard_map/ppermute | solution.py:448
  57.0 2.5 %collective-permute-done.5.c_ref = bf16[64,128]{1,0:T(8,128)(2,1)S(1)} collective-permute-done((bf16[64,128]{1,0:T(8,128)(2,1)S(1)}, bf16[64,128]{1,0:T(8,128)(2,1)S(1)}, u32[]{:S(2)}, u32[]{:S(2)}) %collective-permute-start.5) | collective-permute-done | bytes 16416 | tf_op jit(solution)/shard_map/ppermute | solution.py:448
  59.5 0.0 collective-permute-done.4.b_ref
  59.6 15.8 %all_to_all.16.whole_ref = bf16[8,3,64,128]{3,2,1,0:T(8,128)(2,1)S(1)} all-to-all(bf16[8,3,64,128]{3,2,1,0:T(8,128)(2,1)S(1)} %share.1), channel_id=1, replica_groups={{0,32,64,96,112,16,48,80},{4,36,68,100,116,20,52,84},{8,40,72,104,120,2..., dimensions={0} | all-to-all | bytes 786432 | tf_op jit(solution)/shard_map/all_to_all | solution.py:394
  75.4 0.1 collective-permute-start.7
  75.5 0.7 student_rows.1.rows_ref
  76.2 0.6 collective-permute-done.7.other_ref
  76.8 1.5 %finish.1 = (bf16[1024,128]{1,0:T(8,128)(2,1)}, f32[8,64,128]{2,1,0:T(8,128)}, f32[8,64,128]{2,1,0:T(8,128)}) custom-call(s32[2]{0:T(128)S(1)} %pad_add_fusion.at_ref, bf16[1024,128]{1,0:T(8,128)(2,1)S(1)} %student_rows.1.rows_ref, bf16[8,3,64,128]{3,2,1,0:T(8,128)(2,1)S(1)} %all_to_all.16.whole_ref, bf16[8,64,128]{2,1,0:T(8,128)(2,1)S(1)} %collective-permute-done.7.other_ref), custom_call_target="tpu_custom_call" | custom-call | tf_op jit(solution)/shard_map/finish/pallas_call | solution.py:361
  (6 shorter events, 0.1 us)
Async XLA Ops:
  26.8 14.2 %collective-permute-start.1 = (bf16[8,2,64,256]{3,2,1,0:T(8,128)(2,1)S(1)}, bf16[8,2,64,256]{3,2,1,0:T(8,128)(2,1)S(1)}, u32[]{:S(2)}, u32[]{:S(2)}) collective-permute-start(bf16[8,2,64,256]{3,2,1,0:T(8,128)(2,1)S(1)} %all_to_all.15.token_ref.own_ref), channel_id=1, source_target_pairs={{0,8},{4,12},{8,0},{12,4},{16,24},{20,28},{24,16},{28,20},{32,40},... | collective-permute-start | bytes 1572872 | tf_op jit(solution)/shard_map/ppermute | solution.py:391
  28.3 12.7 %all-to-all-start.1 = ((bf16[8,2,64,128]{3,2,1,0:T(8,128)(2,1)}), bf16[8,2,64,128]{3,2,1,0:T(8,128)(2,1)S(1)}, u32[]{:S(2)}, u32[]{:S(2)}) async-start(bf16[8,2,64,128]{3,2,1,0:T(8,128)(2,1)} %tie.2), calls=%async_computation.1 | async-start | bytes 524288 | tf_op jit(solution)/shard_map/all_to_all | solution.py:394
  31.9 9.2 %collective-permute-start = (bf16[8,2,64,256]{3,2,1,0:T(8,128)(2,1)S(1)}, bf16[8,2,64,256]{3,2,1,0:T(8,128)(2,1)S(1)}, u32[]{:S(2)}, u32[]{:S(2)}) collective-permute-start(bf16[8,2,64,256]{3,2,1,0:T(8,128)(2,1)S(1)} %all_to_all.15.token_ref.own_ref), channel_id=1, source_target_pairs={{0,4},{4,0},{8,12},{12,8},{16,20},{20,16},{24,28},{28,24},{32,36},... | collective-permute-start | bytes 1572872 | tf_op jit(solution)/shard_map/ppermute | solution.py:391
  31.9 9.2 %copy-start = (bf16[8,128,64]{1,2,0:T(8,128)(2,1)S(1)}, bf16[8,128,64]{1,2,0:T(8,128)(2,1)}, u32[]{:S(2)}) copy-start(bf16[8,128,64]{1,2,0:T(8,128)(2,1)} %param.10) | copy-start | bytes 393220
  31.9 9.2 %copy-start.1 = (bf16[8,128,64]{1,2,0:T(8,128)(2,1)S(1)}, bf16[8,128,64]{1,2,0:T(8,128)(2,1)}, u32[]{:S(2)}) copy-start(bf16[8,128,64]{1,2,0:T(8,128)(2,1)} %param.11) | copy-start | bytes 393220
  41.0 3.6 %collective-permute-start.2 = (bf16[8,2,64,256]{3,2,1,0:T(8,128)(2,1)S(1)}, bf16[8,2,64,256]{3,2,1,0:T(8,128)(2,1)S(1)}, u32[]{:S(2)}, u32[]{:S(2)}) collective-permute-start(bf16[8,2,64,256]{3,2,1,0:T(8,128)(2,1)S(1)} %tie.3.x_ref), channel_id=1, source_target_pairs={{0,4},{4,0},{8,12},{12,8},{16,20},{20,16},{24,28},{28,24},{32,36},... | collective-permute-start | bytes 1572872 | tf_op jit(solution)/shard_map/ppermute | solution.py:391
  50.6 1.5 %collective-permute-start.3 = (f32[64,128]{1,0:T(8,128)S(1)}, f32[64,128]{1,0:T(8,128)S(1)}, u32[]{:S(2)}, u32[]{:S(2)}) collective-permute-start(f32[64,128]{1,0:T(8,128)S(1)} %get-tuple-element.39), channel_id=1, source_target_pairs={{0,4},{4,0},{8,12},{12,8},{16,20},{20,16},{24,28},{28,24},{32,36},... | collective-permute-start | bytes 98312 | tf_op jit(solution)/shard_map/ppermute | solution.py:391
  52.1 4.9 %collective-permute-start.6 = (bf16[64,128]{1,0:T(8,128)(2,1)S(1)}, bf16[64,128]{1,0:T(8,128)(2,1)S(1)}, u32[]{:S(2)}, u32[]{:S(2)}) collective-permute-start(bf16[64,128]{1,0:T(8,128)(2,1)S(1)} %pair.1.a_ref), channel_id=1, source_target_pairs={{0,136},{4,140},{8,128},{12,132},{16,152},{20,156},{24,144},{28,14... | collective-permute-start | bytes 49160 | tf_op jit(solution)/shard_map/ppermute | solution.py:448
  54.2 5.4 %collective-permute-start.5 = (bf16[64,128]{1,0:T(8,128)(2,1)S(1)}, bf16[64,128]{1,0:T(8,128)(2,1)S(1)}, u32[]{:S(2)}, u32[]{:S(2)}) collective-permute-start(bf16[64,128]{1,0:T(8,128)(2,1)S(1)} %pair.1.a_ref), channel_id=1, source_target_pairs={{0,128},{4,132},{8,136},{12,140},{16,144},{20,148},{24,152},{28,15... | collective-permute-start | bytes 49160 | tf_op jit(solution)/shard_map/ppermute | solution.py:448
  54.9 4.7 %collective-permute-start.4 = (bf16[64,128]{1,0:T(8,128)(2,1)S(1)}, bf16[64,128]{1,0:T(8,128)(2,1)S(1)}, u32[]{:S(2)}, u32[]{:S(2)}) collective-permute-start(bf16[64,128]{1,0:T(8,128)(2,1)S(1)} %pair.1.a_ref), channel_id=1, source_target_pairs={{0,8},{4,12},{8,0},{12,4},{16,24},{20,28},{24,16},{28,20},{32,40},... | collective-permute-start | bytes 49160 | tf_op jit(solution)/shard_map/ppermute | solution.py:448
  75.4 1.4 %collective-permute-start.7 = (bf16[8,64,128]{2,1,0:T(8,128)(2,1)S(1)}, bf16[8,64,128]{2,1,0:T(8,128)(2,1)S(1)}, u32[]{:S(2)}, u32[]{:S(2)}) collective-permute-start(bf16[8,64,128]{2,1,0:T(8,128)(2,1)S(1)} %slice_bitcast_fusion), channel_id=1, source_target_pairs={{0,4},{4,0},{8,12},{12,8},{16,20},{20,16},{24,28},{28,24},{32,36},... | collective-permute-start | bytes 393224 | tf_op jit(solution)/shard_map/ppermute | solution.py:391
